TPU v7x, 32 devices: a whole 2x2x4 slice. The times are simulated.
32 devices in a mesh: samp: 4 (over y, x), seq: 8 (over z, core).
Axes of the slice: x: 2, y: 2, z: 4, core: 2. Of those that a mesh axis runs over, the one named last changes fastest.
Arguments:
- tokens: bfloat16 [4, 1024, 1024], P('samp', 'seq'), may hold values from -6 to 6
- lead_hours: int32 [4], P('samp'), may hold values from 0 to 168
- var_mask: int32 [4, 48], P('samp'), may hold values 0 or 1
- var_table: bfloat16 [48, 1024], P(None, ('samp', 'seq')), may hold values from -0.875 to 0.875
- lead_weight: bfloat16 [1024], P(('samp', 'seq')), may hold values from -3 to 3
- norm_gain: bfloat16 [2, 1024], P(None, ('samp', 'seq')), may hold values from 0.5 to 1.5
- norm_shift: bfloat16 [2, 1024], P(None, ('samp', 'seq')), may hold values from -2 to 2
- w_qkv: bfloat16 [1024, 3072], P(('samp', 'seq')), may hold values from -0.25 to 0.25
- qv_bias: bfloat16 [2, 1024], P(None, ('samp', 'seq')), may hold values from -2 to 2
- w_out: bfloat16 [1024, 1024], P(('samp', 'seq')), may hold values from -1 to 1
- branch_bias: bfloat16 [2, 1024], P(None, ('samp', 'seq')), may hold values from -2 to 2
- w_up: bfloat16 [1024, 4096], P(('samp', 'seq')), may hold values from -0.1875 to 0.1875
- up_bias: bfloat16 [4096], P(('samp', 'seq')), may hold values from -2 to 2
- w_down: bfloat16 [4096, 1024], P(('samp', 'seq')), may hold values from -0.1875 to 0.1875
- cotangent: bfloat16 [4, 1024, 1024], P('samp', 'seq'), may hold values from -6 to 6
Outputs:
- mixed: bfloat16 [4, 1024, 1024], P('samp', 'seq')
- tokens_grad: float32 [4, 1024, 1024], P('samp', 'seq')
- var_table_grad: float32 [48, 1024], P(None, ('samp', 'seq'))
- lead_weight_grad: float32 [1024], P(('samp', 'seq'))
- norm_gain_grad: float32 [2, 1024], P(None, ('samp', 'seq'))
- norm_shift_grad: float32 [2, 1024], P(None, ('samp', 'seq'))
- w_qkv_grad: float32 [1024, 3072], P(('samp', 'seq'))
- qv_bias_grad: float32 [2, 1024], P(None, ('samp', 'seq'))
- w_out_grad: float32 [1024, 1024], P(('samp', 'seq'))
- branch_bias_grad: float32 [2, 1024], P(None, ('samp', 'seq'))
- w_up_grad: float32 [1024, 4096], P(('samp', 'seq'))
- up_bias_grad: float32 [4096], P(('samp', 'seq'))
- w_down_grad: float32 [4096, 1024], P(('samp', 'seq'))
Inputs may be any that keep to these rules, and one draw needn't show every extreme that they name: `lead_hours`: lead time of each sample in whole hours. `var_mask`: 1 where a sample holds a variable, else 0.
All inputs are finite; a program needn't handle non-finite values. No bound on the sum of `var_mask` on one device may be relied on, other than what follows from the above.
Results may differ from a plain program's by a relative error of at most 0.014.
Values may be sent and summed in bfloat16 or wider, within the bound.
A program may use at most 192 MiB of HBM per device.

v0:
```python
import jax
import jax.numpy as jnp
from jax import lax
from jax.sharding import PartitionSpec as P

HEADS = 16
HEAD_DIM = 64


epsilon = 1e-05
hours_scale = 1.0 / 168.0


def from_behind(block, axis, distance):
    devices = range(lax.axis_size(axis))
    route = [((i - distance) % len(devices), i) for i in devices]
    return lax.ppermute(block, axis, route)


def normalize(field, scaling, offsets):
    average = jnp.mean(field, axis=-1, keepdims=True)
    centred = field - average
    variance = jnp.mean(centred * centred, axis=-1, keepdims=True)
    return centred * lax.rsqrt(variance + epsilon) * scaling + offsets


def block_size(length):
    size_now = length
    while size_now > 512 and size_now % 2 == 0:
        size_now = size_now // 2
    return size_now


def over_blocks(advance, carried, segments):
    length = segments[0].shape[1]
    size_now = block_size(length)
    number = length // size_now
    stacked = tuple(
        (
            jnp.moveaxis(
                segment.reshape(segment.shape[0], number, size_now, segment.shape[2]), 1, 0
            )
            for segment in segments
        )
    )

    def visit(current, blocks):
        return (advance(current, blocks), None)

    carried, _ = lax.scan(visit, carried, stacked)
    return carried


def split_heads(matrix):
    return matrix.reshape(matrix.shape[0], matrix.shape[1], HEADS, HEAD_DIM)


def gelu_slope(upward):
    normal_cdf = 0.5 * (1.0 + lax.erf(upward * 0.7071067811865476))
    density = jnp.exp(-0.5 * upward * upward) * 0.3989422804014327
    return normal_cdf + upward * density


def pair_terms(query_heads, grad_heads, log_total, offset, key_heads, value_heads):
    scores = jnp.einsum(
        "sqhd,skhd->shqk", query_heads, key_heads, preferred_element_type=jnp.float32
    )
    shares = jnp.exp(scores - log_total[..., None])
    pressure = jnp.einsum(
        "sqhd,skhd->shqk", grad_heads, value_heads, preferred_element_type=jnp.float32
    )
    score_grad = (shares * (pressure - offset[..., None])).astype(jnp.bfloat16)
    query_part = jnp.einsum(
        "shqk,skhd->sqhd", score_grad, key_heads, preferred_element_type=jnp.float32
    )
    key_part = jnp.einsum(
        "shqk,sqhd->skhd", score_grad, query_heads, preferred_element_type=jnp.float32
    )
    value_part = jnp.einsum(
        "shqk,sqhd->skhd",
        shares.astype(jnp.bfloat16),
        grad_heads,
        preferred_element_type=jnp.float32,
    )
    return (query_part, key_part, value_part)


def local(
    tokens,
    lead_hours,
    var_mask,
    var_table,
    lead_weight,
    norm_gain,
    norm_shift,
    w_qkv,
    qv_bias,
    w_out,
    branch_bias,
    w_up,
    up_bias,
    w_down,
    cotangent,
):
    samples, patches, features = tokens.shape
    row_count = samples * patches
    factor = HEAD_DIM ** (-0.5)
    (
        table_full,
        lead_full,
        gain_all,
        shift_all,
        qkv_full,
        qv_all,
        out_full,
        bias_all,
        up_full,
        upb_full,
        down_full,
    ) = (
        lax.all_gather(var_table, ("samp", "seq"), axis=1, tiled=True),
        lax.all_gather(lead_weight, ("samp", "seq"), axis=0, tiled=True),
        lax.all_gather(norm_gain, ("samp", "seq"), axis=1, tiled=True),
        lax.all_gather(norm_shift, ("samp", "seq"), axis=1, tiled=True),
        lax.all_gather(w_qkv, ("samp", "seq"), axis=0, tiled=True),
        lax.all_gather(qv_bias, ("samp", "seq"), axis=1, tiled=True),
        lax.all_gather(w_out, ("samp", "seq"), axis=0, tiled=True),
        lax.all_gather(branch_bias, ("samp", "seq"), axis=1, tiled=True),
        lax.all_gather(w_up, ("samp", "seq"), axis=0, tiled=True),
        lax.all_gather(up_bias, ("samp", "seq"), axis=0, tiled=True),
        lax.all_gather(w_down, ("samp", "seq"), axis=0, tiled=True),
    )
    gain_full = gain_all.astype(jnp.float32)
    shift_full = shift_all.astype(jnp.float32)
    qv_full = qv_all.astype(jnp.float32)
    bias_full = bias_all.astype(jnp.float32)
    lead_value = lead_hours.astype(jnp.float32) * hours_scale
    present = var_mask.astype(jnp.float32)
    variable_sum = jnp.dot(present, table_full.astype(jnp.float32), precision=lax.Precision.HIGHEST)
    stream = (
        tokens.astype(jnp.float32)
        + lead_value[:, None, None] * lead_full.astype(jnp.float32)
        + variable_sum[:, None, :]
    )
    stream_rows = stream.reshape(row_count, features)
    normed = normalize(stream_rows, gain_full[0], shift_full[0]).astype(jnp.bfloat16)
    projected = jnp.dot(normed, qkv_full, preferred_element_type=jnp.float32)
    queries = (
        ((projected[:, :features] + qv_full[0]) * factor)
        .astype(jnp.bfloat16)
        .reshape(samples, patches, features)
    )
    keys_all = (
        projected[:, features : 2 * features]
        .astype(jnp.bfloat16)
        .reshape(samples, patches, features)
    )
    values_all = (
        (projected[:, 2 * features :] + qv_full[1])
        .astype(jnp.bfloat16)
        .reshape(samples, patches, features)
    )
    query_heads = split_heads(queries)

    def scores_of(keys_block):
        return jnp.einsum(
            "sqhd,skhd->shqk",
            query_heads,
            split_heads(keys_block),
            preferred_element_type=jnp.float32,
        )

    def stats_step(carried, blocks):
        running_max, running_sum = carried
        scores = scores_of(blocks[0])
        new_max = jnp.maximum(running_max, jnp.max(scores, axis=-1))
        running_sum = running_sum * jnp.exp(running_max - new_max) + jnp.sum(
            jnp.exp(scores - new_max[..., None]), axis=-1
        )
        return (new_max, running_sum)

    stats_start = (
        jnp.full((samples, HEADS, patches), -jnp.inf, jnp.float32),
        jnp.zeros((samples, HEADS, patches), jnp.float32),
    )
    running_max, running_sum = over_blocks(
        stats_step, stats_start, (lax.all_gather(keys_all, "seq", axis=1, tiled=True),)
    )
    log_total = running_max + jnp.log(running_sum)

    def mix_step(collected, blocks):
        shares = jnp.exp(scores_of(blocks[0]) - log_total[..., None]).astype(jnp.bfloat16)
        return collected + jnp.einsum(
            "shqk,skhd->sqhd", shares, split_heads(blocks[1]), preferred_element_type=jnp.float32
        )

    zero_heads = jnp.zeros((samples, patches, HEADS, HEAD_DIM), jnp.float32)
    attended_f = over_blocks(
        mix_step,
        zero_heads,
        (
            lax.all_gather(keys_all, "seq", axis=1, tiled=True),
            lax.all_gather(values_all, "seq", axis=1, tiled=True),
        ),
    )
    attended = attended_f.reshape(row_count, features).astype(jnp.bfloat16)
    middle = stream_rows + (
        jnp.dot(attended, out_full, preferred_element_type=jnp.float32) + bias_full[0]
    )
    normed_two = normalize(middle, gain_full[1], shift_full[1]).astype(jnp.bfloat16)
    upward = jnp.dot(normed_two, up_full, preferred_element_type=jnp.float32) + upb_full.astype(
        jnp.float32
    )
    activated = jax.nn.gelu(upward, approximate=False).astype(jnp.bfloat16)
    downward = jnp.dot(activated, down_full, preferred_element_type=jnp.float32) + bias_full[1]
    mixed = (middle + downward).astype(jnp.bfloat16).reshape(samples, patches, features)
    gain_back, qkv_back, out_back, up_back, down_back = (
        lax.all_gather(norm_gain, ("samp", "seq"), axis=1, tiled=True),
        lax.all_gather(w_qkv, ("samp", "seq"), axis=0, tiled=True),
        lax.all_gather(w_out, ("samp", "seq"), axis=0, tiled=True),
        lax.all_gather(w_up, ("samp", "seq"), axis=0, tiled=True),
        lax.all_gather(w_down, ("samp", "seq"), axis=0, tiled=True),
    )
    gain_back = gain_back.astype(jnp.float32)
    incoming = cotangent.astype(jnp.float32).reshape(row_count, features)
    incoming_low = incoming.astype(jnp.bfloat16)
    down_grad = jnp.einsum("tf,td->fd", activated, incoming_low, preferred_element_type=jnp.float32)
    down_bias_grad = jnp.sum(incoming_low.astype(jnp.float32), axis=0)
    gelu_grad = jnp.einsum(
        "td,fd->tf", incoming_low, down_back, preferred_element_type=jnp.float32
    ) * gelu_slope(upward)
    up_low = gelu_grad.astype(jnp.bfloat16)
    up_grad = jnp.einsum("td,tf->df", normed_two, up_low, preferred_element_type=jnp.float32)
    up_bias_grad = jnp.sum(up_low.astype(jnp.float32), axis=0)
    normed_two_grad = jnp.einsum("tf,df->td", up_low, up_back, preferred_element_type=jnp.float32)
    _, pull_second = jax.vjp(normalize, middle, gain_back[1], shift_full[1])
    middle_part, gain_two_grad, shift_two_grad = pull_second(normed_two_grad)
    middle_grad = incoming + middle_part
    middle_low = middle_grad.astype(jnp.bfloat16)
    out_grad = jnp.einsum("te,td->ed", attended, middle_low, preferred_element_type=jnp.float32)
    out_bias_grad = jnp.sum(middle_low.astype(jnp.float32), axis=0)
    attended_grad = jnp.einsum(
        "td,ed->te", middle_low, out_back, preferred_element_type=jnp.float32
    ).astype(jnp.bfloat16)
    grad_rows = attended_grad.reshape(samples, patches, features)
    grad_heads = split_heads(grad_rows)
    offset = jnp.transpose(jnp.sum(grad_heads.astype(jnp.float32) * attended_f, axis=-1), (0, 2, 1))
    grads_start = jnp.zeros((2, samples, patches, HEADS, HEAD_DIM), jnp.float32)

    def visit_block(blocks, partial_grads, query_acc):
        query_part, key_part, value_part = pair_terms(
            query_heads,
            grad_heads,
            log_total,
            offset,
            split_heads(blocks[0]),
            split_heads(blocks[1]),
        )
        return (partial_grads + jnp.stack([key_part, value_part]), query_acc + query_part)

    def turn_grads(partial_grads):
        return from_behind(partial_grads.astype(jnp.bfloat16), "seq", 1).astype(partial_grads.dtype)

    def cycle_step(counter, carried):
        blocks, partial_grads, query_acc = carried
        partial_grads, query_acc = visit_block(blocks, partial_grads, query_acc)
        partial_grads = turn_grads(partial_grads)
        blocks = from_behind(blocks, "seq", 1)
        return (blocks, partial_grads, query_acc)

    blocks_start = jnp.stack([keys_all, values_all])
    blocks, partial_grads, query_acc = lax.fori_loop(
        0, lax.axis_size("seq") - 1, cycle_step, (blocks_start, grads_start, zero_heads)
    )
    partial_grads, query_acc = visit_block(blocks, partial_grads, query_acc)
    partial_grads = turn_grads(partial_grads)
    query_low = query_acc.astype(jnp.bfloat16).reshape(row_count, features) * factor
    key_low = partial_grads[0].astype(jnp.bfloat16).reshape(row_count, features)
    value_low = partial_grads[1].astype(jnp.bfloat16).reshape(row_count, features)
    proj_grad = jnp.concatenate([query_low, key_low, value_low], axis=1)
    qkv_grad = jnp.einsum("td,te->de", normed, proj_grad, preferred_element_type=jnp.float32)
    qv_bias_grad = jnp.stack(
        [
            jnp.sum(query_low.astype(jnp.float32), axis=0),
            jnp.sum(value_low.astype(jnp.float32), axis=0),
        ]
    )
    normed_grad = jnp.einsum("te,de->td", proj_grad, qkv_back, preferred_element_type=jnp.float32)
    _, pull_first = jax.vjp(normalize, stream_rows, gain_back[0], shift_full[0])
    stream_part, gain_one_grad, shift_one_grad = pull_first(normed_grad)
    stream_grad = (middle_grad + stream_part).reshape(samples, patches, features)
    per_sample = jnp.sum(stream_grad, axis=1)
    lead_grad = jnp.sum(lead_value[:, None] * per_sample, axis=0)
    table_grad = jnp.dot(present.T, per_sample, precision=lax.Precision.HIGHEST)
    gain_grad = jnp.stack([gain_one_grad, gain_two_grad])
    shift_grad = jnp.stack([shift_one_grad, shift_two_grad])
    bias_grad = jnp.stack([out_bias_grad, down_bias_grad])
    owned = (
        lax.psum_scatter(table_grad, ("samp", "seq"), scatter_dimension=1, tiled=True),
        lax.psum_scatter(lead_grad, ("samp", "seq"), scatter_dimension=0, tiled=True),
        lax.psum_scatter(gain_grad, ("samp", "seq"), scatter_dimension=1, tiled=True),
        lax.psum_scatter(shift_grad, ("samp", "seq"), scatter_dimension=1, tiled=True),
        lax.psum_scatter(qkv_grad, ("samp", "seq"), scatter_dimension=0, tiled=True),
        lax.psum_scatter(qv_bias_grad, ("samp", "seq"), scatter_dimension=1, tiled=True),
        lax.psum_scatter(out_grad, ("samp", "seq"), scatter_dimension=0, tiled=True),
        lax.psum_scatter(bias_grad, ("samp", "seq"), scatter_dimension=1, tiled=True),
        lax.psum_scatter(up_grad, ("samp", "seq"), scatter_dimension=0, tiled=True),
        lax.psum_scatter(up_bias_grad, ("samp", "seq"), scatter_dimension=0, tiled=True),
        lax.psum_scatter(down_grad, ("samp", "seq"), scatter_dimension=0, tiled=True),
    )
    return (
        mixed,
        stream_grad,
        owned[0],
        owned[1],
        owned[2],
        owned[3],
        owned[4],
        owned[5],
        owned[6],
        owned[7],
        owned[8],
        owned[9],
        owned[10],
    )


def solution(mesh):
    return jax.shard_map(
        local,
        mesh=mesh,
        in_specs=(
            P("samp", "seq", None),
            P("samp"),
            P("samp", None),
            P(None, ("samp", "seq")),
            P(("samp", "seq")),
            P(None, ("samp", "seq")),
            P(None, ("samp", "seq")),
            P(("samp", "seq"), None),
            P(None, ("samp", "seq")),
            P(("samp", "seq"), None),
            P(None, ("samp", "seq")),
            P(("samp", "seq"), None),
            P(("samp", "seq")),
            P(("samp", "seq"), None),
            P("samp", "seq", None),
        ),
        out_specs=(
            P("samp", "seq", None),
            P("samp", "seq", None),
            P(None, ("samp", "seq")),
            P(("samp", "seq")),
            P(None, ("samp", "seq")),
            P(None, ("samp", "seq")),
            P(("samp", "seq"), None),
            P(None, ("samp", "seq")),
            P(("samp", "seq"), None),
            P(None, ("samp", "seq")),
            P(("samp", "seq"), None),
            P(("samp", "seq")),
            P(("samp", "seq"), None),
        ),
        check_vma=False,
    )
```

profile of v0, /device:TPU:0, one launch (start us, length us, event | category | flops | bytes accessed | tf_op | source)
XLA Modules:
  0.0 1979.6 jit_solution(7548025557350409933)
XLA Ops:
  8.0 43.2 %all-gather.3 = bf16[32,32,2]{1,2,0:T(2,128)(2,1)S(1)} all-gather(bf16[1,32,2]{1,2,0:T(2,128)(2,1)} %bitcast.379), channel_id=1, replica_groups=mesh['samp'=4,'seq'=8] {'samp','seq'}, dimensions={0}, use_global_device_ids=true | all-gather | bytes 4224 | tf_op jit(solution)/shard_map/all_gather | solution.py:124
  51.3 36.8 %all-gather.2 = bf16[32,32,2]{1,2,0:T(2,128)(2,1)S(1)} all-gather(bf16[1,32,2]{1,2,0:T(2,128)(2,1)} %bitcast.380), channel_id=1, replica_groups=mesh['samp'=4,'seq'=8] {'samp','seq'}, dimensions={0}, use_global_device_ids=true | all-gather | bytes 4224 | tf_op jit(solution)/shard_map/all_gather | solution.py:123
  89.7 39.5 %all-reduce = bf16[1024]{0:T(1024)(128)(2,1)S(1)} all-reduce(bf16[1024]{0:T(1024)(128)(2,1)S(1)} %dynamic-update-slice), channel_id=1, replica_groups=mesh['samp'=4,'seq'=8] {'samp','seq'}, use_global_device_ids=true, to_apply=%add | all-reduce | flops 1024 | bytes 4096
  129.1 40.7 %all_gather.46 = bf16[48,1024]{0,1:T(8,128)(2,1)S(1)} all-gather(bf16[48,32]{0,1:T(8,128)(2,1)} %param.24), channel_id=1, replica_groups=mesh['samp'=4,'seq'=8] {'samp','seq'}, dimensions={1}, use_global_device_ids=true | all-gather | bytes 101376 | tf_op jit(solution)/shard_map/all_gather | solution.py:121
  178.0 36.7 %all-gather.4 = bf16[32,32,2]{1,2,0:T(2,128)(2,1)S(1)} all-gather(bf16[1,32,2]{1,2,0:T(2,128)(2,1)S(1)} %bitcast.381), channel_id=1, replica_groups=mesh['samp'=4,'seq'=8] {'samp','seq'}, dimensions={0}, use_global_device_ids=true | all-gather | bytes 4224 | tf_op jit(solution)/shard_map/all_gather | solution.py:126
  217.5 38.1 %all-gather.5 = bf16[32,32,2]{1,2,0:T(2,128)(2,1)S(1)} all-gather(bf16[1,32,2]{1,2,0:T(2,128)(2,1)S(1)} %bitcast.382), channel_id=1, replica_groups=mesh['samp'=4,'seq'=8] {'samp','seq'}, dimensions={0}, use_global_device_ids=true | all-gather | bytes 4224 | tf_op jit(solution)/shard_map/all_gather | solution.py:128
  255.7 36.9 %all-gather.6 = bf16[32,1,128]{2,1,0:T(2,128)(2,1)S(1)} all-gather(bf16[1,1,128]{2,1,0:T(2,128)(2,1)S(1)} %bitcast.383), channel_id=1, replica_groups=mesh['samp'=4,'seq'=8] {'samp','seq'}, dimensions={0}, use_global_device_ids=true | all-gather | bytes 8448 | tf_op jit(solution)/shard_map/all_gather | solution.py:130
  296.8 11.4 while.39
  308.2 12.3 while.40
  324.1 57.1 %all-gather.18.cloned.1.call-done = bf16[1024,4096]{1,0:T(8,128)(2,1)} async-done(((bf16[32,4096]{1,0:T(8,128)(2,1)}), bf16[1024,4096]{1,0:T(8,128)(2,1)}) %all-gather.18.cloned.1.call-update) | async-done | bytes 8388624 | tf_op jit(solution)/shard_map/all_gather | solution.py:129
  385.9 74.1 %all-gather.20.cloned.1.call-done = bf16[4096,1024]{1,0:T(8,128)(2,1)} async-done(((bf16[128,1024]{1,0:T(8,128)(2,1)}), bf16[4096,1024]{1,0:T(8,128)(2,1)}) %all-gather.20.cloned.1.call-update) | async-done | bytes 8388624 | tf_op jit(solution)/shard_map/all_gather | solution.py:131
  472.8 139.9 %while.41 = (s32[]{:T(128)}, bf16[2,1,128,1024]{2,3,1,0:T(8,128)(2,1)S(1)}, f32[2,1,128,16,64]{2,4,3,1,0:T(8,128)}, f32[1,128,16,64]{1,3,2,0:T(8,128)S(1)}, bf16...) while((s32[]{:T(128)}, ...), condition=%wide.region_14.15_spmd.clone, body=%wide.region_13.14_spmd.clone.sunk | while | flops 170655744 | bytes 19153088 | solution.py:272
  477.8 8.5 collective-permute-done.1
  496.3 10.1 collective-permute-done.1
  516.4 10.1 collective-permute-done.1
  536.6 10.1 collective-permute-done.1
  556.7 10.1 collective-permute-done.1
  576.8 10.1 collective-permute-done.1
  596.9 10.1 collective-permute-done.1
  615.7 9.7 collective-permute-done.2
  658.4 9.7 fusion.54
  668.2 8.6 fusion.43
  676.8 37.0 %all-reduce.3 = (f32[1024]{0:T(1024)S(1)}, f32[4096]{0:T(1024)S(1)}) all-reduce(f32[1024]{0:T(1024)S(1)} %broadcast_multiply_fusion, f32[4096]{0:T(1024)S(1)} %get-tuple-element.341), channel_id=5, replica_groups=mesh['samp'=4,'seq'=8] {'samp','seq'}, use_global_device_ids=true, to_apply=%region_19.20.clone | all-reduce | flops 5120 | bytes 40960
  715.0 49.5 %reduce-scatter.28.cloned.1.call-done = f32[32,2]{1,0:T(8,128)} async-done(((f32[1024,2]{1,0:T(8,128)}), f32[32,2]{1,0:T(8,128)}) %reduce-scatter.28.cloned.1.call-update) | async-done | bytes 272
  765.9 131.2 %reduce-scatter.30.cloned.1.call-done = f32[32,2]{1,0:T(8,128)} async-done(((f32[1024,2]{1,0:T(8,128)}), f32[32,2]{1,0:T(8,128)}) %reduce-scatter.30.cloned.1.call-update) | async-done | bytes 272
  898.5 131.7 %reduce-scatter.32.cloned.1.call-done = f32[32,2]{1,0:T(8,128)} async-done(((f32[1024,2]{1,0:T(8,128)}), f32[32,2]{1,0:T(8,128)}) %reduce-scatter.32.cloned.1.call-update) | async-done | bytes 272
  1031.5 131.0 %reduce-scatter.34.cloned.1.call-done = f32[32,2]{1,0:T(8,128)} async-done(((f32[1024,2]{1,0:T(8,128)}), f32[32,2]{1,0:T(8,128)}) %reduce-scatter.34.cloned.1.call-update) | async-done | bytes 272
  1163.9 131.9 %reduce-scatter.18.cloned.1.call-done = f32[48,32]{0,1:T(8,128)} async-done(((f32[48,1024]{0,1:T(8,128)}), f32[48,32]{0,1:T(8,128)}) %reduce-scatter.18.cloned.1.call-update) | async-done | bytes 6160 | tf_op jit(solution)/shard_map/reduce_scatter | solution.py:299
  1295.8 141.7 %reduce-scatter.22.cloned.1.call-done = f32[32,1024]{1,0:T(8,128)} async-done(((f32[1024,1024]{1,0:T(8,128)}), f32[32,1024]{1,0:T(8,128)}) %reduce-scatter.22.cloned.1.call-update) | async-done | bytes 131088 | tf_op jit(solution)/shard_map/reduce_scatter | solution.py:305
  1437.5 159.8 %reduce-scatter.20.cloned.1.call-done = f32[32,3072]{1,0:T(8,128)} async-done(((f32[1024,3072]{1,0:T(8,128)}), f32[32,3072]{1,0:T(8,128)}) %reduce-scatter.20.cloned.1.call-update) | async-done | bytes 393232 | tf_op jit(solution)/shard_map/reduce_scatter | solution.py:303
  1597.3 188.5 %reduce-scatter.24.cloned.1.call-done = f32[32,4096]{1,0:T(8,128)} async-done(((f32[1024,4096]{1,0:T(8,128)}), f32[32,4096]{1,0:T(8,128)}) %reduce-scatter.24.cloned.1.call-update) | async-done | bytes 524304 | tf_op jit(solution)/shard_map/reduce_scatter | solution.py:307
  1785.7 187.1 %reduce-scatter.26.cloned.1.call-done = f32[128,1024]{1,0:T(8,128)} async-done(((f32[4096,1024]{1,0:T(8,128)}), f32[128,1024]{1,0:T(8,128)}) %reduce-scatter.26.cloned.1.call-update) | async-done | bytes 524304 | tf_op jit(solution)/shard_map/reduce_scatter | solution.py:309
  (277 shorter events, 173.7 us)
Async XLA Ops:
  7.2 166.0 %all-gather.14.cloned.1.call-start = ((), (), s32[]{:S(2)}) async-start(), calls=%async_computation.9 | async-start | bytes 6488064 | tf_op jit(solution)/shard_map/all_gather | solution.py:125
  7.9 286.0 %all-gather.24.cloned.1.call-start = ((), (), s32[]{:S(2)}) async-start(), calls=%async_computation.19 | async-start | bytes 2359296 | tf_op jit(solution)/shard_map/all_gather | solution.py:202
  177.9 130.3 %all-gather.22.cloned.1.call-start = ((), (), s32[]{:S(2)}) async-start(), calls=%async_computation.18 | async-start | bytes 2359296 | tf_op jit(solution)/shard_map/all_gather | solution.py:203
  215.7 106.0 %all-gather.16.cloned.1.call-start = ((), (), s32[]{:S(2)}) async-start(), calls=%async_computation.10 | async-start | bytes 2162688 | tf_op jit(solution)/shard_map/all_gather | solution.py:127
  216.2 164.9 %all-gather.18.cloned.1.call-start = ((), (), s32[]{:S(2)}) async-start(), calls=%async_computation.11 | async-start | bytes 8650752 | tf_op jit(solution)/shard_map/all_gather | solution.py:129
  216.8 243.2 %all-gather.20.cloned.1.call-start = ((), (), s32[]{:S(2)}) async-start(), calls=%async_computation.12 | async-start | bytes 8650752 | tf_op jit(solution)/shard_map/all_gather | solution.py:131
  217.4 547.2 %reduce-scatter.28.cloned.1.call-start = ((), (), s32[]{:S(2)}) async-start(), calls=%async_computation.20 | async-start | bytes 540672
  323.9 145.9 %copy-start.3 = (f32[128,1024]{1,0:T(8,128)}, f32[128,1024]{1,0:T(8,128)S(1)}, u32[]{:S(2)}) copy-start(f32[128,1024]{1,0:T(8,128)S(1)} %get-tuple-element.338) | copy-start | bytes 1572868
  385.9 80.7 %copy-start.17 = (f32[128,4096]{1,0:T(8,128)}, f32[128,4096]{1,0:T(8,128)S(1)}, u32[]{:S(2)}) copy-start(f32[128,4096]{1,0:T(8,128)S(1)} %convolution_add_fusion) | copy-start | bytes 6291460
  475.7 10.6 collective-permute-start.1
  476.0 16.0 collective-permute-start
  495.8 10.6 collective-permute-start.1
  495.8 16.2 collective-permute-start
  516.0 10.6 collective-permute-start.1
  516.0 16.2 collective-permute-start
  536.1 10.6 collective-permute-start.1
  536.1 16.2 collective-permute-start
  556.2 10.6 collective-permute-start.1
  556.2 16.2 collective-permute-start
  576.3 10.6 collective-permute-start.1
  576.3 16.2 collective-permute-start
  596.5 10.6 collective-permute-start.1
  596.5 16.2 collective-permute-start
  614.9 10.5 collective-permute-start.2
  633.2 263.9 %reduce-scatter.30.cloned.1.call-start = ((), (), s32[]{:S(2)}) async-start(), calls=%async_computation.21 | async-start | bytes 540672
  634.7 395.5 %reduce-scatter.32.cloned.1.call-start = ((), (), s32[]{:S(2)}) async-start(), calls=%async_computation.22 | async-start | bytes 540672
  635.8 526.7 %reduce-scatter.34.cloned.1.call-start = ((), (), s32[]{:S(2)}) async-start(), calls=%async_computation.23 | async-start | bytes 540672
  636.9 658.9 %reduce-scatter.18.cloned.1.call-start = ((), (), s32[]{:S(2)}) async-start(), calls=%async_computation.13 | async-start | bytes 540672 | tf_op jit(solution)/shard_map/reduce_scatter | solution.py:299
  638.0 799.4 %reduce-scatter.22.cloned.1.call-start = ((), (), s32[]{:S(2)}) async-start(), calls=%async_computation.15 | async-start | bytes 4325376 | tf_op jit(solution)/shard_map/reduce_scatter | solution.py:305
  640.8 956.5 %reduce-scatter.20.cloned.1.call-start = ((), (), s32[]{:S(2)}) async-start(), calls=%async_computation.14 | async-start | bytes 12976128 | tf_op jit(solution)/shard_map/reduce_scatter | solution.py:303
  647.3 1138.4 %reduce-scatter.24.cloned.1.call-start = ((), (), s32[]{:S(2)}) async-start(), calls=%async_computation.16 | async-start | bytes 17301504 | tf_op jit(solution)/shard_map/reduce_scatter | solution.py:307
  656.9 1316.0 %reduce-scatter.26.cloned.1.call-start = ((), (), s32[]{:S(2)}) async-start(), calls=%async_computation.17 | async-start | bytes 17301504 | tf_op jit(solution)/shard_map/reduce_scatter | solution.py:309
  (24 other events, 400.0 us)
Sparse Core Ops, SparseCore 0:
  11.0 72.1 all-gather.13
  178.1 26.5 all-gather.23
  215.8 27.4 all-gather.21
  246.1 56.0 all-gather.15
  305.0 76.1 all-gather.17
  384.0 75.9 all-gather.19
  633.4 131.1 reduce-scatter.27
  766.9 130.1 reduce-scatter.29
  899.4 130.7 reduce-scatter.31
  1032.3 130.1 reduce-scatter.33
  1165.4 130.3 reduce-scatter.17
  1298.6 138.8 reduce-scatter.21
  1445.1 152.1 reduce-scatter.19
  1600.0 185.7 reduce-scatter.23
  1788.5 184.3 reduce-scatter.25
where the time goes:
time: 1980 us
  waiting for transfers between devices  1500 us (76%)
  blocking collectives  309 us (16%)
  matrix products  92 us (5%)
  other arithmetic  35.7 us (2%)
  local copies, waits for them, and re-layouts  27.8 us (1%)
    unnamed x19, waiting for transfers between devices  446 us
    reduce_scatter x1, waiting for transfers between devices, local(): lax.psum_scatter(up_grad, ('samp', 'seq'), scatter_dimension=0, tiled=True)  188 us
    reduce_scatter x1, waiting for transfers between devices, local(): lax.psum_scatter(down_grad, ('samp', 'seq'), scatter_dimension=0, tiled=T...  187 us
    reduce_scatter x1, waiting for transfers between devices, local(): lax.psum_scatter(qkv_grad, ('samp', 'seq'), scatter_dimension=0, tiled=True)  160 us
    reduce_scatter x1, waiting for transfers between devices, local(): lax.psum_scatter(out_grad, ('samp', 'seq'), scatter_dimension=0, tiled=True)  142 us
    reduce_scatter x1, waiting for transfers between devices, local(): lax.psum_scatter(table_grad, ('samp', 'seq'), scatter_dimension=1, tiled=...  132 us
    ppermute x15, waiting for transfers between devices, from_behind(): return lax.ppermute(block, axis, route)  111 us
    unnamed x2, blocking collectives  76.5 us
  transfers between devices with their start and end apart: 30, of which 26 were waited for; matrix products, arithmetic and copies ran while one was open for 5% of the time, Pallas kernels for 0%

commit v1 on v0

--- a/solution.py
+++ b/solution.py
@@ -1,6 +1,8 @@
 import jax
 import jax.numpy as jnp
 from jax import lax
+from jax.experimental import pallas as pl
+from jax.experimental.pallas import tpu as pltpu
 from jax.sharding import PartitionSpec as P
 
 HEADS = 16
@@ -325,9 +327,792 @@
     )
 
 
+MESH = pl.DeviceIdType.MESH
+BF = jnp.bfloat16
+F32 = jnp.float32
+D = 1024
+ROWS = 128
+LANES = 8
+FFL = 512
+
+
+def dot_nn(a, b):
+    return lax.dot_general(a, b, (((1,), (0,)), ((), ())), preferred_element_type=F32)
+
+
+def dot_nt(a, b):
+    return lax.dot_general(a, b, (((1,), (1,)), ((), ())), preferred_element_type=F32)
+
+
+def dot_tn(a, b):
+    return lax.dot_general(a, b, (((0,), (0,)), ((), ())), preferred_element_type=F32)
+
+
+def erf(v):
+    v = jnp.clip(v, -4.0, 4.0)
+    s = v * v
+    p = jnp.full_like(s, -2.72614225801306e-10)
+    for a in (2.77068142495902e-08, -2.10102402082508e-06, -5.69250639462346e-05,
+              -7.34990630326855e-04, -2.95459980854025e-03, -1.60960333262415e-02):
+        p = p * s + a
+    q = jnp.full_like(s, -1.45660718464996e-05)
+    for b in (-2.13374055278905e-04, -1.68282697438203e-03, -7.37332916720468e-03, -1.42647390514189e-02):
+        q = q * s + b
+    return v * p / q
+
+
+def flip(a, d):
+    return 1 - a if d else a
+
+
+def many(n, m=1):
+    return pl.ds(pl.multiple_of(n, m), m)
+
+
+def center(v):
+    mean = jnp.mean(v, axis=-1, keepdims=True)
+    centred = v - mean
+    var = jnp.mean(centred * centred, axis=-1, keepdims=True)
+    rstd = lax.rsqrt(var + epsilon)
+    return centred * rstd, rstd
+
+
+def norm_back(xhat, rstd, gain, grad):
+    dx = grad * gain
+    return rstd * (dx - jnp.mean(dx, axis=-1, keepdims=True) - xhat * jnp.mean(dx * xhat, axis=-1, keepdims=True))
+
+
+def fast_kernel(
+    tokens, cot, wqkv_in, wout_in, wup_in, wdown_in, pack_in,
+    mixed_o, tg_o, gq_o, go_o, gu_o, gd_o, small_o,
+    tok_all, cot_all, n2_all, ml_all,
+    wqkv, wup, wdown, wout, pack_all, full,
+    normed, q_s, k_s, v_s, shares, attf, att,
+    rs_s1, rs_r1, rs_s2, rs_r2, own,
+    middle, mgrad, act, uplow, dproj, dog, dk_acc, dv_acc,
+    gqkv, gup, gdown, gout, rqkv, rup, rdown, rout, sq2, su2, rq2, ru2, so2, ro2,
+    tgs, tgr, smallp, s_a, r_a, s_b, r_b, r_c, upb_g, r_upb,
+    ss, rs,
+):
+    s_i = lax.axis_index("samp")
+    q_i = lax.axis_index("seq")
+    y, x = s_i // 2, s_i % 2
+    z, c = q_i // 2, q_i % 2
+    k, w = z // 2, z % 2
+    idx = 16 * y + 8 * x + 4 * k + 2 * w + c
+    lane = 4 * y + 2 * w + c
+    rank = 2 * x + k
+    sample = 2 * k + x
+    off_diag = y + k - 2 * y * k
+    is_home = 1 - (x + w - 2 * x * w) - (k + c - 2 * k * c) + (x + w - 2 * x * w) * (k + c - 2 * k * c)
+    my_rows = many(ROWS * lane, ROWS)
+
+    def dev(y_, x_, k_, w_, c_):
+        return (2 * y_ + x_, 4 * k_ + 2 * w_ + c_)
+
+    count = [0, 0]
+    pending = []
+
+    def sems(n):
+        a, b = count
+        count[0] += n
+        count[1] += n
+        return a, b
+
+    def rc(src, dst, a, b, device):
+        return pltpu.make_async_remote_copy(src_ref=src, dst_ref=dst, send_sem=ss.at[a], recv_sem=rs.at[b], device_id=device, device_id_type=MESH)
+
+    group = [(d // 4, (d // 2) % 2, d % 2) for d in range(1, 8)]
+    chips = [(0, 0), (0, 1), (1, 0), (1, 1)]
+    ranks = [(0, 1), (1, 0), (1, 1)]
+
+    def peer(d):
+        dy, dw, dc = d
+        y_, w_, c_ = flip(y, dy), flip(w, dw), flip(c, dc)
+        return y_, w_, c_, 4 * y_ + 2 * w_ + c_, dev(y_, x, k, w_, c_)
+
+    def partner(d):
+        dx, dk = d
+        x_, k_ = flip(x, dx), flip(k, dk)
+        return x_, k_, 2 * x_ + k_, dev(y, x_, k_, w, c)
+
+    swap_dev = dev(k, x, y, w, c)
+
+    barrier = pltpu.get_barrier_semaphore()
+    for d in group:
+        pl.semaphore_signal(barrier, inc=1, device_id=peer(d)[4], device_id_type=MESH)
+    for d in ranks:
+        pl.semaphore_signal(barrier, inc=1, device_id=partner(d)[3], device_id_type=MESH)
+
+    @pl.when(off_diag == 1)
+    def _():
+        pl.semaphore_signal(barrier, inc=1, device_id=swap_dev, device_id_type=MESH)
+
+    pl.semaphore_wait(barrier, 10 + off_diag)
+
+    def swap_start(src, dst, a, b):
+        @pl.when(off_diag == 1)
+        def _():
+            rc(src, dst, a, b, swap_dev).start()
+
+    def swap_wait(src, dst, a, b):
+        @pl.when(off_diag == 1)
+        def _():
+            rc(src, dst, a, b, swap_dev).wait()
+
+    class Gather:
+        def __init__(self, buf):
+            self.buf = buf
+            self.a, self.b = sems(8)
+
+        def copy(self, i, forward):
+            dy, dw = chips[i]
+            if i == 0:
+                return rc(self.buf.at[my_rows], self.buf.at[my_rows], self.a, self.b, peer((0, 0, 1))[4])
+            y_, w_, c_, l_, dv = peer((dy, dw, 0))
+            if forward:
+                rows = many(ROWS * l_, ROWS)
+                return rc(self.buf.at[rows], self.buf.at[rows], self.a + 4 + i, self.b + 4 + i, peer((0, 0, 1))[4])
+            return rc(self.buf.at[my_rows], self.buf.at[my_rows], self.a + i, self.b + i, dv)
+
+        def start(self):
+            for i in (3, 1, 2, 0):
+                self.copy(i, False).start()
+
+        def pass_on(self):
+            for i in (1, 2, 3):
+                self.copy(i, False).wait_recv()
+                self.copy(i, True).start()
+
+        def finish(self):
+            self.copy(0, False).wait_recv()
+            for i in (1, 2, 3):
+                self.copy(i, True).wait_recv()
+
+        def drain(self):
+            for i in range(4):
+                self.copy(i, False).wait_send()
+            for i in (1, 2, 3):
+                self.copy(i, True).wait_send()
+
+    class Scatter:
+        def __init__(self, slot, partial):
+            self.slot = slot
+            self.partial = partial
+            self.a1, self.b1 = sems(4)
+            self.a2, self.b2 = sems(4)
+
+        def far(self, i):
+            dy, dw = i // 2, i % 2
+            y_, w_ = y + dy - 2 * y * dy, w + dw - 2 * w * dw
+            return y_, w_
+
+        def first(self, i):
+            return rc(rs_s1.at[self.slot, i], rs_r1.at[self.slot, i], self.a1 + i, self.b1 + i, dev(y, x, k, w, 1 - c))
+
+        def second(self, i):
+            y_, w_ = self.far(i)
+            return rc(rs_s2.at[self.slot, i - 1], rs_r2.at[self.slot, i - 1], self.a2 + i, self.b2 + i, dev(y_, x, k, w_, c))
+
+        def start(self):
+            @pl.loop(0, 4)
+            def _(n):
+                i = 3 - n
+                y_, w_ = self.far(i)
+                rs_s1[self.slot, i] = self.partial(4 * y_ + 2 * w_ + 1 - c).astype(BF)
+                self.first(i).start()
+
+            @pl.loop(0, 4)
+            def _(n):
+                i = 3 - n
+                y_, w_ = self.far(i)
+                part = self.partial(4 * y_ + 2 * w_ + c)
+                self.first(i).wait_recv()
+                total = part + rs_r1[self.slot, i].astype(F32)
+
+                @pl.when(i > 0)
+                def _():
+                    rs_s2[self.slot, i - 1] = total.astype(BF)
+                    self.second(i).start()
+
+                @pl.when(i == 0)
+                def _():
+                    own[self.slot] = total
+
+        def finish(self):
+            for i in (1, 2, 3):
+                self.second(i).wait_recv()
+            total = own[self.slot]
+            for i in (1, 2, 3):
+                total = total + rs_r2[self.slot, i - 1].astype(F32)
+            return total
+
+        def drain(self):
+            for i in range(4):
+                self.first(i).wait_send()
+            for i in (1, 2, 3):
+                self.second(i).wait_send()
+
+    class Batch:
+        def __init__(self, copies):
+            self.copies = copies
+            self.a, self.b = sems(len(copies))
+
+        def copy(self, n):
+            src, dst, device = self.copies[n]
+            return rc(src, dst, self.a + n, self.b + n, device)
+
+        def start(self):
+            for n in range(len(self.copies)):
+                self.copy(n).start()
+
+        def wait(self):
+            for n in range(len(self.copies)):
+                self.copy(n).wait_recv()
+
+        def drain(self):
+            for n in range(len(self.copies)):
+                self.copy(n).wait_send()
+
+    tok_swap = sems(1)
+    cot_swap = sems(1)
+    swap_rows = many(ROWS * (4 * k + 2 * w + c), ROWS)
+    swap_start(tokens, tok_all.at[swap_rows], *tok_swap)
+
+    own_rows = many(32 * idx, 32)
+    copies = []
+    for d in group:
+        y_, w_, c_, l_, dv = peer(d)
+        copies.append((pack_in, pack_all.at[idx], dv))
+        for p in range(3):
+            copies.append((wqkv_in.at[:, many(128 * (8 * p + l_), 128)], wqkv.at[own_rows, pl.ds(128 * p, 128)], dv))
+    in_qkv = Batch(copies)
+    copies = []
+    for d in group:
+        y_, w_, c_, l_, dv = peer(d)
+        for r in range(4):
+            copies.append((wup_in.at[:, many(128 * (16 * y_ + 8 * (r // 2) + 4 * (r % 2) + 2 * w_ + c_), 128)], wup.at[own_rows, pl.ds(128 * r, 128)], dv))
+    in_up = Batch(copies)
+    in_qkv.start()
+    cot_send = cot
+
+    @pl.when(off_diag == 0)
+    def _():
+        tok_all[my_rows, :] = tokens[...]
+
+    pack_all[idx] = pack_in[...]
+    for p in range(3):
+        wqkv[own_rows, 128 * p : 128 * p + 128] = wqkv_in[:, many(128 * (8 * p + lane), 128)]
+
+    swap_wait(tokens, tok_all.at[swap_rows], *tok_swap)
+    tok = Gather(tok_all)
+    tok.start()
+
+    out_a, out_b = sems(4)
+    place = 2 * w + c
+    out_rows = many(32 * place, 32)
+    home_dev = dev(y, x, k, x, k)
+    send_out = rc(wout_in, wout.at[out_rows], out_a, out_b + place, home_dev)
+
+    @pl.when(is_home == 0)
+    def _():
+        send_out.start()
+
+    @pl.when(is_home == 1)
+    def _():
+        wout[out_rows, :] = wout_in[...]
+
+    in_qkv.wait()
+
+    def between(pieces):
+        copies = []
+        for d in ranks:
+            x_, k_, r_, dv = partner(d)
+            for ref in pieces:
+                copies.append((ref, ref, dv))
+        return Batch(copies)
+
+    base = 16 * 0 + 8 * x + 4 * k
+    pack_pieces = [pack_all.at[pl.ds(base + 16 * y_, 4)] for y_ in range(2)]
+    qkv_pieces = [wqkv.at[many(512 * y_ + 256 * x + 128 * k, 128)] for y_ in range(2)]
+    up_pieces = [wup.at[many(512 * y_ + 256 * x + 128 * k, 128)] for y_ in range(2)]
+    rank_rows = many(128 * rank, 128)
+    dp_qkv = between(pack_pieces + qkv_pieces)
+    dp_qkv.start()
+    in_up.start()
+    for r in range(4):
+        wup[own_rows, 128 * r : 128 * r + 128] = wup_in[:, many(128 * (16 * y + 8 * (r // 2) + 4 * (r % 2) + 2 * w + c), 128)]
+    wdown[rank_rows, :] = wdown_in[...]
+
+    dpo_a, dpo_b = sems(3)
+    dp_out = [rc(wout, wout, dpo_a + n, dpo_b, partner(d)[3]) for n, d in enumerate(ranks)]
+
+    @pl.when(is_home == 1)
+    def _():
+        for dw, dc in ((0, 1), (1, 0), (1, 1)):
+            m = 2 * flip(w, dw) + flip(c, dc)
+            rows = many(32 * m, 32)
+            rc(wout_in, wout.at[rows], out_a, out_b + m, home_dev).wait_recv()
+        for copy in dp_out:
+            copy.start()
+
+    tok.pass_on()
+    swap_start(cot, cot_all.at[swap_rows], *cot_swap)
+
+    @pl.when(off_diag == 0)
+    def _():
+        cot_all[my_rows, :] = cot[...]
+
+    in_up.wait()
+    dp_up = between(up_pieces)
+    dp_up.start()
+    dp_down = Batch([(wdown_in, wdown.at[rank_rows], partner(d)[3]) for d in ranks])
+    dp_down.start()
+
+    dp_qkv.wait()
+    lane_id = lax.broadcasted_iota(jnp.int32, (16, 128), 1)
+    for b in range(8):
+        for t in range(4):
+            block = None
+            for m in range(4):
+                piece = pack_all[4 * b + m].astype(F32)
+                shift = (32 * (m - t)) % 128
+                if shift:
+                    piece = pltpu.roll(piece, shift, 1)
+                block = piece if block is None else jnp.where(lane_id // 32 == m, piece, block)
+            full[16 * t : 16 * t + 16, 128 * b : 128 * b + 128] = block
+
+    gain0, gain1 = full[54:55, :], full[55:56, :]
+    shift0, shift1 = full[56:57, :], full[57:58, :]
+    lane_cols = many(128 * lane, 128)
+    bias_q, bias_v = full[58:59, lane_cols], full[59:60, lane_cols]
+    bias_out, bias_down = full[60:61, :], full[61:62, :]
+    bias_up = jnp.concatenate(
+        [pack_all[16 * y + 8 * (r // 2) + 4 * (r % 2) + 2 * w + c].astype(F32)[15:16, :] for r in range(4)], axis=1
+    )
+    facts = pack_all[8 * sample].astype(F32)[14:15, :]
+    one_lane = lax.broadcasted_iota(jnp.int32, (1, 128), 1)
+    present = jnp.where(one_lane < 64, facts, 0.0)
+    hours = jnp.sum(jnp.where(one_lane == 64, facts, 0.0), axis=-1, keepdims=True) * hours_scale
+    present8 = jnp.broadcast_to(present, (8, 128))[:, :64].astype(BF)
+    extra = dot_nn(present8, full[...].astype(BF))[0:1, :] + hours * full[62:63, :]
+
+    tok.finish()
+
+    @pl.loop(0, 8)
+    def _(n):
+        rows = many(128 * n, 128)
+        xhat, _ = center(tok_all[rows, :].astype(F32) + extra)
+        normed[rows, :] = (xhat * gain0 + shift0).astype(BF)
+
+    @pl.loop(0, 4)
+    def _(n):
+        rows = many(256 * n, 256)
+        proj = dot_nn(normed[rows, :], wqkv[...])
+        q_s[rows, :] = ((proj[:, :128] + bias_q) * 0.125).astype(BF)
+        k_s[rows, :] = proj[:, 128:256].astype(BF)
+        v_s[rows, :] = (proj[:, 256:384] + bias_v).astype(BF)
+
+    QB = 256
+    head_lane = lax.broadcasted_iota(jnp.int32, (1, 128), 1) // 64
+
+    def of_head(v, h):
+        return jnp.where(head_lane == h, v, jnp.zeros_like(v))
+
+    @pl.loop(0, D // QB)
+    def _(n):
+        rows = many(QB * n, QB)
+        queries = q_s[rows, :]
+        total = None
+        for h in range(2):
+            scores = dot_nt(of_head(queries, h), k_s[...])
+            top = jnp.max(scores, axis=-1, keepdims=True)
+            e = jnp.exp(scores - top)
+            share = (e * (1.0 / jnp.sum(e, axis=-1, keepdims=True))).astype(BF)
+            shares[h, rows, :] = share
+            got = of_head(dot_nn(share, v_s[...]), h)
+            total = got if total is None else total + got
+        attf[rows, :] = total
+        att[rows, :] = total.astype(BF)
+
+    @pl.when(is_home == 0)
+    def _():
+        rc(wout, wout, dpo_a, dpo_b, home_dev).wait_recv()
+
+    def rows_of(l_):
+        return many(ROWS * l_, ROWS)
+
+    rs_out = Scatter(0, lambda l_: dot_nn(att[rows_of(l_), :], wout[...]))
+    rs_out.start()
+
+    swap_wait(cot, cot_all.at[swap_rows], *cot_swap)
+    cg = Gather(cot_all)
+    cg.start()
+
+    stream = tok_all[my_rows, :].astype(F32) + extra
+    mid = stream + (rs_out.finish() + bias_out)
+    middle[...] = mid
+    xhat2, rstd2 = center(mid)
+    n2_all[my_rows, :] = (xhat2 * gain1 + shift1).astype(BF)
+    n2 = Gather(n2_all)
+    n2.start()
+    cg.pass_on()
+    n2.pass_on()
+    dp_up.wait()
+    dp_down.wait()
+    cg.finish()
+    n2.finish()
+
+    upb_g[...] = jnp.zeros_like(upb_g)
+
+    @pl.loop(0, 8)
+    def _(n):
+        rows = many(128 * n, 128)
+        up = dot_nn(n2_all[rows, :], wup[...]) + bias_up
+        cdf = 0.5 * (1.0 + erf(up * 0.7071067811865476))
+        act[rows, :] = (up * cdf).astype(BF)
+        slope = cdf + up * (jnp.exp(-0.5 * up * up) * 0.3989422804014327)
+        low = (dot_nt(cot_all[rows, :], wdown[...]) * slope).astype(BF)
+        uplow[rows, :] = low
+        upb_g[0:1, :] += jnp.sum(low.astype(F32), axis=0, keepdims=True)
+
+    rs_n2 = Scatter(1, lambda l_: dot_nt(uplow[rows_of(l_), :], wup[...]))
+    rs_n2.start()
+    rs_mix = Scatter(2, lambda l_: dot_nn(act[rows_of(l_), :], wdown[...]))
+    rs_mix.start()
+
+    n2_grad = rs_n2.finish()
+    incoming = cot_all[my_rows, :].astype(F32)
+    xhat2, rstd2 = center(middle[...])
+    mg = incoming + norm_back(xhat2, rstd2, gain1, n2_grad)
+    mgrad[...] = mg
+    ml_all[my_rows, :] = mg.astype(BF)
+    ml = Gather(ml_all)
+    ml.start()
+    smallp[2:3, :] = jnp.sum(n2_grad * xhat2, axis=0, keepdims=True)
+    smallp[4:5, :] = jnp.sum(n2_grad, axis=0, keepdims=True)
+    smallp[5:6, :] = jnp.sum(mg.astype(BF).astype(F32), axis=0, keepdims=True)
+    smallp[6:7, :] = jnp.sum(incoming, axis=0, keepdims=True)
+
+    @pl.loop(0, 4)
+    def _(r):
+        cols = many(128 * r, 128)
+        gdown[cols, :] = dot_tn(act[:, cols], cot_all[...]).astype(BF)
+
+    down_sends = Batch([(gdown.at[many(128 * partner(d)[2], 128)], rdown.at[n], partner(d)[3]) for n, d in enumerate(ranks)])
+    down_sends.start()
+    upb_sends_src = upb_g
+    upb_sends = Batch([(upb_g.at[:, many(128 * partner(d)[2], 128)], r_upb.at[n], partner(d)[3]) for n, d in enumerate(ranks)])
+    upb_sends.start()
+    ml.pass_on()
+
+    @pl.loop(0, 4)
+    def _(n):
+        cols = many(256 * n, 256)
+        gup[cols, :] = dot_tn(n2_all[:, cols], uplow[...]).astype(BF)
+
+    def spread(src, recv):
+        copies = []
+        for n, d in enumerate(ranks):
+            x_, k_, r_, dv = partner(d)
+            for y_ in range(2):
+                copies.append((src.at[many(512 * y_ + 256 * x_ + 128 * k_, 128)], recv.at[n, pl.ds(128 * y_, 128)], dv))
+        return Batch(copies)
+
+    up_sends = spread(gup, rup)
+    up_sends.start()
+    ml.finish()
+
+    @pl.loop(0, 4)
+    def _(n):
+        rows = many(256 * n, 256)
+        dog[rows, :] = dot_nt(ml_all[rows, :], wout[...]).astype(BF)
+
+    dk_acc[...] = jnp.zeros_like(dk_acc)
+    dv_acc[...] = jnp.zeros_like(dv_acc)
+
+    @pl.loop(0, D // QB)
+    def _(n):
+        rows = many(QB * n, QB)
+        queries = q_s[rows, :]
+        grads = dog[rows, :]
+        both = grads.astype(F32) * attf[rows, :]
+        dq = None
+        for h in range(2):
+            share = shares[h, rows, :]
+            pressure = dot_nt(of_head(grads, h), v_s[...])
+            offset = jnp.sum(of_head(both, h), axis=-1, keepdims=True)
+            ds = (share.astype(F32) * (pressure - offset)).astype(BF)
+            got = of_head(dot_nn(ds, k_s[...]), h)
+            dq = got if dq is None else dq + got
+            dk_acc[...] += dot_tn(ds, of_head(queries, h))
+            dv_acc[...] += dot_tn(share, of_head(grads, h))
+        dproj[rows, 0:128] = (dq.astype(BF).astype(F32) * 0.125).astype(BF)
+
+    dproj[:, 128:256] = dk_acc[...].astype(BF)
+    dproj[:, 256:384] = dv_acc[...].astype(BF)
+
+    rs_n1 = Scatter(3, lambda l_: dot_nt(dproj[rows_of(l_), :], wqkv[...]))
+    rs_n1.start()
+
+    @pl.loop(0, 4)
+    def _(n):
+        cols = many(256 * n, 256)
+        gqkv[cols, :] = dot_tn(normed[:, cols], dproj[...]).astype(BF)
+
+    qkv_sends = spread(gqkv, rqkv)
+    qkv_sends.start()
+
+    n1_grad = rs_n1.finish()
+    xhat1, rstd1 = center(tok_all[my_rows, :].astype(F32) + extra)
+    tg = mgrad[...] + norm_back(xhat1, rstd1, gain0, n1_grad)
+    tgs[...] = tg
+    tg_swap = sems(1)
+    tgs_b = tgr.at[0]
+    tgr[0] = tg.astype(BF)
+    swap_start(tgr.at[0], tgr.at[1], *tg_swap)
+    smallp[0:1, :] = jnp.sum(tg, axis=0, keepdims=True)
+    smallp[1:2, :] = jnp.sum(n1_grad * xhat1, axis=0, keepdims=True)
+    smallp[3:4, :] = jnp.sum(n1_grad, axis=0, keepdims=True)
+    smallp[7:8, :] = jnp.zeros((1, D), F32)
+
+    gout[...] = dot_tn(att[...], ml_all[...]).astype(BF)
+    go_a, go_b = sems(4)
+    hx, hk = x + w - 2 * x * w, k + c - 2 * k * c
+    apart = 2 * hx + hk
+    send_home = rc(gout, rout.at[apart], go_a, go_b + apart, dev(y, w, c, w, c))
+
+    @pl.when(is_home == 0)
+    def _():
+        send_home.start()
+
+    small_group = Batch([(smallp.at[:, many(128 * peer(d)[3], 128)], r_a.at[n], peer(d)[4]) for n, d in enumerate(group)])
+    small_group.start()
+
+    mix_swap = sems(1)
+    mixed_low = (middle[...] + (rs_mix.finish() + bias_down)).astype(BF)
+    tgr[2] = mixed_low
+    swap_start(tgr.at[2], tgr.at[3], *mix_swap)
+
+    small_group.wait()
+    total = smallp[:, lane_cols]
+    for n in range(7):
+        total = total + r_a[n]
+    s_b[0:8, :] = total
+    low = dproj[...].astype(F32)
+    s_b[8:9, :] = jnp.sum(low[:, 0:128], axis=0, keepdims=True)
+    s_b[9:10, :] = jnp.sum(low[:, 256:384], axis=0, keepdims=True)
+    s_b[10:16, :] = jnp.zeros((6, 128), F32)
+    small_ranks = Batch([(s_b, r_b.at[n], partner(d)[3]) for n, d in enumerate(ranks)])
+    small_ranks.start()
+
+    down_sends.wait()
+    sum_down = gdown[rank_rows, :].astype(F32)
+    for n in range(3):
+        sum_down = sum_down + rdown[n].astype(F32)
+    gd_o[...] = sum_down
+    mine = [many(512 * y_ + 256 * x + 128 * k, 128) for y_ in range(2)]
+
+    def collect(src, recv, low_sum):
+        for y_ in range(2):
+            part = src[mine[y_], :].astype(F32)
+            for n in range(3):
+                part = part + recv[n, 128 * y_ : 128 * y_ + 128, :].astype(F32)
+            low_sum[128 * y_ : 128 * y_ + 128, :] = part.astype(BF)
+
+    def deal(low_sum, recv):
+        copies = []
+        for n, d in enumerate(group):
+            y_, w_, c_, l_, dv = peer(d)
+            copies.append((low_sum.at[many(128 * y_ + 64 * w_ + 32 * c_, 32)], recv.at[lane], dv))
+        return Batch(copies)
+
+    my_deal = many(128 * y + 64 * w + 32 * c, 32)
+    up_sends.wait()
+    collect(gup, rup, su2)
+    up_deal = deal(su2, ru2)
+    up_deal.start()
+    ru2[lane] = su2[my_deal, :]
+
+    @pl.when(is_home == 1)
+    def _():
+        for n, d in enumerate(ranks):
+            slot = 2 * d[0] + d[1]
+            rc(gout, rout.at[slot], go_a, go_b + slot, partner(d)[3]).wait_recv()
+        sum_out = gout[...].astype(F32)
+        for slot in range(1, 4):
+            sum_out = sum_out + rout[slot].astype(F32)
+        so2[...] = sum_out.astype(BF)
+
+    outs_a, outs_b = sems(3)
+    home_copies = []
+    for n, (dw, dc) in enumerate(((0, 1), (1, 0), (1, 1))):
+        w_, c_ = flip(w, dw), flip(c, dc)
+        home_copies.append(rc(so2.at[many(32 * (2 * w_ + c_), 32)], ro2, outs_a + n, outs_b, dev(y, x, k, w_, c_)))
+
+    @pl.when(is_home == 1)
+    def _():
+        for copy in home_copies:
+            copy.start()
+        go_o[...] = so2[out_rows, :].astype(F32)
+
+    qkv_sends.wait()
+    collect(gqkv, rqkv, sq2)
+    qkv_deal = deal(sq2, rq2)
+    qkv_deal.start()
+    rq2[lane] = sq2[my_deal, :]
+
+    small_ranks.wait()
+    blocks = [None] * 4
+    rows_sum = s_b[...]
+    for n in range(3):
+        rows_sum = rows_sum + r_b[n]
+    own_facts = [facts] + [pack_all[8 * (2 * partner(d)[1] + partner(d)[0])].astype(F32)[14:15, :] for d in ranks]
+    own_sums = [s_b[0:1, :]] + [r_b[n, 0:1, :] for n in range(3)]
+    facts8 = jnp.concatenate(own_facts + [jnp.zeros((4, 128), F32)], axis=0)
+    facts_t = jnp.transpose(facts8)
+    table = None
+    for n in range(4):
+        part = facts_t[:, n : n + 1] * own_sums[n]
+        table = part if table is None else table + part
+    s_a[0:64, :] = table[0:64, :]
+    s_a[64:80, :] = rows_sum
+    s_a[80:81, :] = table[64:65, :] * hours_scale
+    s_a[81:88, :] = jnp.zeros((7, 128), F32)
+    sm_a, sm_b = sems(3)
+    small_copies = []
+    for n, (dw, dc) in enumerate(((0, 1), (1, 0), (1, 1))):
+        w_, c_ = flip(w, dw), flip(c, dc)
+        small_copies.append(rc(s_a, r_c, sm_a + n, sm_b, dev(y, x, k, w_, c_)))
+
+    @pl.when(is_home == 1)
+    def _():
+        for copy in small_copies:
+            copy.start()
+        small_o[0:88, :] = s_a[...]
+
+    @pl.when(is_home == 0)
+    def _():
+        rc(s_a, r_c, sm_a, sm_b, home_dev).wait_recv()
+        small_o[0:88, :] = r_c[...]
+
+    upb_sends.wait()
+    sum_upb = upb_g[:, rank_rows]
+    for n in range(3):
+        sum_upb = sum_upb + r_upb[n]
+    small_o[88:96, :] = sum_upb
+
+    @pl.when(is_home == 0)
+    def _():
+        rc(so2.at[pl.ds(0, 32)], ro2, outs_a, outs_b, home_dev).wait_recv()
+        go_o[...] = ro2[...].astype(F32)
+
+    @pl.when(off_diag == 0)
+    def _():
+        tg_o[...] = tgs[...]
+        mixed_o[...] = tgr[2]
+
+    swap_wait(tgr.at[2], tgr.at[3], *mix_swap)
+    swap_wait(tgr.at[0], tgr.at[1], *tg_swap)
+
+    @pl.when(off_diag == 1)
+    def _():
+        tg_o[...] = tgr[1].astype(F32)
+        mixed_o[...] = tgr[3]
+
+    up_deal.wait()
+    for l_ in range(8):
+        part = ru2[l_].astype(F32)
+        y_, w_, c_ = l_ // 4, (l_ // 2) % 2, l_ % 2
+        for r in range(4):
+            at = 128 * (16 * y_ + 8 * (r // 2) + 4 * (r % 2) + 2 * w_ + c_)
+            gu_o[:, at : at + 128] = part[:, 128 * r : 128 * r + 128]
+    qkv_deal.wait()
+    for l_ in range(8):
+        part = rq2[l_].astype(F32)
+        for p in range(3):
+            at = 128 * (8 * p + l_)
+            gq_o[:, at : at + 128] = part[:, 128 * p : 128 * p + 128]
+
+    for item in (in_qkv, in_up, dp_qkv, dp_up, dp_down, tok, cg, n2, ml, rs_out, rs_n2, rs_mix, rs_n1,
+                 down_sends, upb_sends, up_sends, qkv_sends, small_group, small_ranks, up_deal, qkv_deal):
+        item.drain()
+
+    @pl.when(is_home == 0)
+    def _():
+        send_out.wait_send()
+        send_home.wait_send()
+
+    @pl.when(is_home == 1)
+    def _():
+        for copy in dp_out + home_copies + small_copies:
+            copy.wait_send()
+
+
+def local_fast(
+    tokens, lead_hours, var_mask, var_table, lead_weight, norm_gain, norm_shift, w_qkv, qv_bias, w_out,
+    branch_bias, w_up, up_bias, w_down, cotangent,
+):
+    mask = var_mask.astype(BF)[0]
+    zero = jnp.zeros((1, 2), BF)
+    parts = [mask[14 * t : min(14 * t + 14, 48)] for t in range(4)]
+    slots = jnp.concatenate([parts[0], zero[0], parts[1], zero[0], parts[2], zero[0], parts[3], jnp.zeros((10,), BF)])
+    hours = jnp.concatenate([lead_hours.astype(BF), jnp.zeros((31,), BF)])
+    ub = up_bias.reshape(4, 32)
+    rows = jnp.concatenate(
+        [
+            var_table[0:14], slots[None, 0:32], ub[0:1],
+            var_table[14:28], slots[None, 32:64], ub[1:2],
+            var_table[28:42], hours[None], ub[2:3],
+            var_table[42:48], norm_gain, norm_shift, qv_bias, branch_bias, lead_weight[None], ub[3:4],
+        ],
+        axis=0,
+    )
+    pack = rows.reshape(4, 16, 32).transpose(1, 0, 2).reshape(16, 128)
+
+    vm = pltpu.VMEM
+    scratch = [
+        vm((D, D), BF), vm((D, D), BF), vm((D, D), BF), vm((D, D), BF),
+        vm((D, 384), BF), vm((D, FFL), BF), vm((FFL, D), BF), vm((128, D), BF), vm((32, 16, 128), BF), vm((64, D), F32),
+        vm((D, D), BF), vm((D, 128), BF), vm((D, 128), BF), vm((D, 128), BF), vm((2, D, D), BF), vm((D, 128), F32), vm((D, 128), BF),
+        vm((4, 4, 128, D), BF), vm((4, 4, 128, D), BF), vm((4, 3, 128, D), BF), vm((4, 3, 128, D), BF), vm((4, 128, D), F32),
+        vm((128, D), F32), vm((128, D), F32), vm((D, FFL), BF), vm((D, FFL), BF), vm((D, 384), BF), vm((D, 128), BF), vm((D, 128), F32), vm((D, 128), F32),
+        vm((D, 384), BF), vm((D, FFL), BF), vm((FFL, D), BF), vm((128, D), BF),
+        vm((3, 256, 384), BF), vm((3, 256, FFL), BF), vm((3, 128, D), BF), vm((4, 128, D), BF),
+        vm((256, 384), BF), vm((256, FFL), BF), vm((8, 32, 384), BF), vm((8, 32, FFL), BF), vm((128, D), BF), vm((32, D), BF),
+        vm((128, D), F32), vm((4, 128, D), BF), vm((8, D), F32), vm((88, 128), F32), vm((7, 8, 128), F32), vm((16, 128), F32), vm((3, 16, 128), F32), vm((88, 128), F32),
+        vm((8, FFL), F32), vm((3, 8, 128), F32),
+        pltpu.SemaphoreType.DMA((260,)), pltpu.SemaphoreType.DMA((260,)),
+    ]
+    outs = [
+        jax.ShapeDtypeStruct((128, D), BF), jax.ShapeDtypeStruct((128, D), F32), jax.ShapeDtypeStruct((32, 3 * D), F32),
+        jax.ShapeDtypeStruct((32, D), F32), jax.ShapeDtypeStruct((32, 4 * D), F32), jax.ShapeDtypeStruct((128, D), F32),
+        jax.ShapeDtypeStruct((96, 128), F32),
+    ]
+    mixed, tg, gq, go, gu, gd, small = pl.pallas_call(
+        fast_kernel,
+        out_shape=outs,
+        in_specs=[pl.BlockSpec(memory_space=vm)] * 7,
+        out_specs=[pl.BlockSpec(memory_space=vm)] * 7,
+        scratch_shapes=scratch,
+        compiler_params=pltpu.CompilerParams(collective_id=0, has_side_effects=True, vmem_limit_bytes=62 * 2**20),
+        cost_estimate=pl.CostEstimate(flops=14_000_000_000, bytes_accessed=4_000_000, transcendentals=6_000_000),
+    )(tokens[0], cotangent[0], w_qkv, w_out, w_up, w_down, pack)
+    place = lax.axis_index("seq") % 4
+    mine = lax.dynamic_slice(small, (0, 32 * place), (88, 32))
+    table = jnp.concatenate([mine[0:14], mine[16:30], mine[32:46], mine[48:54]], axis=0)
+    tail = mine[64:80]
+    return (
+        mixed[None], tg[None], table, mine[80],
+        tail[1:3], tail[3:5], gq, tail[8:10], go, tail[5:7], gu, small[88], gd,
+    )
+
+
 def solution(mesh):
+    sizes = dict(mesh.shape)
+    fast = sizes == {"samp": 4, "seq": 8}
     return jax.shard_map(
-        local,
+        local_fast if fast else local,
         mesh=mesh,
         in_specs=(
             P("samp", "seq", None),

time: 1980 us -> 280 us (0.14)
  waiting for transfers between devices: 1500 us -> 0 us
  blocking collectives: 309 us -> 0 us
  Pallas kernels: 0 us -> 261 us
  matrix products: 92 us -> 0 us
  other arithmetic: 35.7 us -> 0.1 us
    reduce_scatter x5 -> x0, waiting for transfers between devices: 809 us -> none  [the longest x1 188 us: local(): lax.psum_scatter(up_grad, ('samp', 'seq'), scatter_dimension=0, tiled=True)]
    unnamed x19 -> x0, waiting for transfers between devices: 446 us -> none
    pallas_call x0 -> x1, Pallas kernels: none -> 261 us  [local_fast(): pl.pallas_call(fast_kernel, out_shape=outs, in_specs=[pl.BlockSpec(memory...]
    all_gather x6 -> x0, blocking collectives: 232 us -> none  [the longest x1 43.2 us: local(): lax.all_gather(norm_shift, ('samp', 'seq'), axis=1, tiled=True)]
    all_gather x6 -> x0, waiting for transfers between devices: 131 us -> none  [the longest x1 74.1 us: local(): lax.all_gather(w_down, ('samp', 'seq'), axis=0, tiled=True)]
    ppermute x15 -> x0, waiting for transfers between devices: 111 us -> none  [from_behind(): return lax.ppermute(block, axis, route)]
    dot_general x57 -> x0, matrix products: 92 us -> none  [the longest x1 9.7 us: local(): jnp.einsum('tf,td->fd', activated, incoming_low, preferred_element_type=j...]
    unnamed x2 -> x0, blocking collectives: 76.5 us -> none
  transfers between devices with their start and end apart: 30 -> 0, of which waited for: 26 -> 0; matrix products, arithmetic and copies ran while one was open for 5% -> 0% of each run, Pallas kernels for 0% -> 0%
where the time goes in v1:
time: 280 us; the launch traced here: 279 us
  Pallas kernels  261 us (93%)
  local copies, waits for them, and re-layouts  16.3 us (6%)
    pallas_call x1, Pallas kernels, local_fast(): pl.pallas_call(fast_kernel, out_shape=outs, in_specs=[pl.BlockSpec(memory...  261 us
    unnamed x37, local copies, waits for them, and re-layouts  9.5 us

profile of v1, /device:TPU:0, one launch (start us, length us, event | category | flops | bytes accessed | tf_op | source)
XLA Modules:
  0.0 279.1 jit_solution(980542171955154624)
XLA Ops:
  0.7 0.6 copy-done.12
  1.3 0.1 slice_bitcast_fusion.5
  1.4 0.1 slice_bitcast_fusion.4
  1.5 0.1 fusion.4
  2.3 0.1 slice_bitcast_fusion.1
  2.3 0.6 copy-done.4
  2.9 0.1 fusion.7
  3.0 0.1 copy.48
  3.1 0.1 copy.49
  3.2 0.1 copy.50
  3.3 0.1 slice.116
  3.4 0.1 copy.51
  3.5 0.6 copy-done.10
  4.0 0.1 copy-done.7
  4.2 0.2 concatenate.19
  4.4 0.7 reshape.42.pack_in
  5.0 261.3 %shard_map.246 = (bf16[128,1024]{1,0:T(8,128)(2,1)}, f32[128,1024]{1,0:T(8,128)}, f32[32,3072]{1,0:T(8,128)}, f32[32,1024]{1,0:T(8,128)}, f32[32,4096]{1,0:T(8,1...) custom-call(bf16[128,1024]{1,0:T(8,128)(2,1)} %bitcast.38, bf16[128,1024]{1,0:T(8,128)(2,1)} %bitcast.39, ...), custom_call_target="tpu_custom_call" | custom-call | flops 14000000000 | bytes 4000000 | tf_op jit(solution)/shard_map/pallas_call | solution.py:1092
  266.3 0.9 constant_dynamic-slice_fusion
  267.2 0.8 dynamic-slice.3
  268.0 0.7 copy.47
  268.6 1.4 fusion.6
  270.1 1.3 dynamic-slice_bitcast_fusion
  271.3 1.2 slice_bitcast_fusion
  272.5 1.7 copy.59
  274.2 0.8 copy.60
  275.0 0.4 copy-done.3
  275.4 0.7 copy.61
  276.1 0.2 copy-done.5
  276.4 0.7 copy.62
  277.0 0.8 copy.63
  277.8 0.4 copy-done
  278.3 0.8 copy.64
  (24 shorter events, 0.1 us)
Async XLA Ops:
  0.7 0.7 copy-start.12
  1.6 0.7 copy-start.6
  2.2 0.7 copy-start.4
  3.4 0.7 copy-start.10
  3.4 0.7 copy-start.11
  3.5 0.7 copy-start.7
  3.5 0.7 copy-start.8
  3.5 0.7 copy-start.9
  266.3 7.9 %copy-start.2 = (f32[128,1024]{1,0:T(8,128)S(1)}, f32[128,1024]{1,0:T(8,128)}, u32[]{:S(2)}) copy-start(f32[128,1024]{1,0:T(8,128)} %get-tuple-element.21) | copy-start | bytes 1572868
  274.2 1.2 copy-start.3
  275.4 1.0 copy-start.5
  275.4 1.7 copy-start.1
  277.0 1.2 copy-start

commit v2 on v1

--- a/solution.py
+++ b/solution.py
@@ -383,15 +383,17 @@
 
 
 def fast_kernel(
-    tokens, cot, wqkv_in, wout_in, wup_in, wdown_in, pack_in,
+    tokens, lead_hours, var_mask, var_table, lead_weight, norm_gain, norm_shift, wqkv_in, qv_bias, wout_in,
+    branch_bias, wup_in, up_bias, wdown_in, cot,
     mixed_o, tg_o, gq_o, go_o, gu_o, gd_o, small_o,
     tok_all, cot_all, n2_all, ml_all,
-    wqkv, wup, wdown, wout, pack_all, full,
+    wqkv, wup, wdown, wout, raw, pack_in, pack_all, full,
     normed, q_s, k_s, v_s, shares, attf, att,
     rs_s1, rs_r1, rs_s2, rs_r2, own,
     middle, mgrad, act, uplow, dproj, dog, dk_acc, dv_acc,
-    gqkv, gup, gdown, gout, rqkv, rup, rdown, rout, sq2, su2, rq2, ru2, so2, ro2,
-    tgs, tgr, smallp, s_a, r_a, s_b, r_b, r_c, upb_g, r_upb,
+    gqkv, gup, gdown, gout, xqkv, xup, xdown, zqkv_s, zup_s, zdown_s, zqkv, zup, zdown,
+    out_x, out_s, out_z, sq2, su2, rq2, ru2, so2, ro2,
+    tgr, smallp, s_a, r_a, s_b, r_b, r_c, upb_g, r_upb,
     ss, rs,
 ):
     s_i = lax.axis_index("samp")
@@ -411,7 +413,7 @@
         return (2 * y_ + x_, 4 * k_ + 2 * w_ + c_)
 
     count = [0, 0]
-    pending = []
+    items = []
 
     def sems(n):
         a, b = count
@@ -450,15 +452,52 @@
 
     pl.semaphore_wait(barrier, 10 + off_diag)
 
-    def swap_start(src, dst, a, b):
-        @pl.when(off_diag == 1)
-        def _():
-            rc(src, dst, a, b, swap_dev).start()
-
-    def swap_wait(src, dst, a, b):
-        @pl.when(off_diag == 1)
-        def _():
-            rc(src, dst, a, b, swap_dev).wait()
+    def begun(item):
+        items.append(item)
+        item.got = False
+
+    class Swap:
+        def __init__(self, src, dst):
+            self.copy = rc(src, dst, *sems(1), swap_dev)
+
+        def start(self):
+            begun(self)
+            pl.when(off_diag == 1)(self.copy.start)
+
+        def wait(self):
+            self.got = True
+            pl.when(off_diag == 1)(self.copy.wait_recv)
+
+        def drain(self):
+            pl.when(off_diag == 1)(self.copy.wait_send)
+
+    class Only:
+        def __init__(self, sends, outgoing, takes, incoming):
+            self.sends, self.outgoing, self.takes, self.incoming = sends, outgoing, takes, incoming
+
+        def each(self, flag, copies, name):
+            @pl.when(flag == 1)
+            def _():
+                for copy in copies:
+                    getattr(copy, name)()
+
+        def start(self):
+            begun(self)
+            self.each(self.sends, self.outgoing, "start")
+
+        def wait(self):
+            self.got = True
+            self.each(self.takes, self.incoming, "wait_recv")
+
+        def drain(self):
+            self.each(self.sends, self.outgoing, "wait_send")
+
+    def finish_all():
+        for item in items:
+            if not item.got:
+                item.wait()
+        for item in items:
+            item.drain()
 
     class Gather:
         def __init__(self, buf):
@@ -476,15 +515,21 @@
             return rc(self.buf.at[my_rows], self.buf.at[my_rows], self.a + i, self.b + i, dv)
 
         def start(self):
+            begun(self)
+            self.passed = False
             for i in (3, 1, 2, 0):
                 self.copy(i, False).start()
 
         def pass_on(self):
+            self.passed = True
             for i in (1, 2, 3):
                 self.copy(i, False).wait_recv()
                 self.copy(i, True).start()
 
-        def finish(self):
+        def wait(self):
+            if not self.passed:
+                self.pass_on()
+            self.got = True
             self.copy(0, False).wait_recv()
             for i in (1, 2, 3):
                 self.copy(i, True).wait_recv()
@@ -515,6 +560,8 @@
             return rc(rs_s2.at[self.slot, i - 1], rs_r2.at[self.slot, i - 1], self.a2 + i, self.b2 + i, dev(y_, x, k, w_, c))
 
         def start(self):
+            begun(self)
+
             @pl.loop(0, 4)
             def _(n):
                 i = 3 - n
@@ -539,7 +586,8 @@
                 def _():
                     own[self.slot] = total
 
-        def finish(self):
+        def wait(self):
+            self.got = True
             for i in (1, 2, 3):
                 self.second(i).wait_recv()
             total = own[self.slot]
@@ -563,10 +611,12 @@
             return rc(src, dst, self.a + n, self.b + n, device)
 
         def start(self):
+            begun(self)
             for n in range(len(self.copies)):
                 self.copy(n).start()
 
         def wait(self):
+            self.got = True
             for n in range(len(self.copies)):
                 self.copy(n).wait_recv()
 
@@ -574,10 +624,115 @@
             for n in range(len(self.copies)):
                 self.copy(n).wait_send()
 
-    tok_swap = sems(1)
-    cot_swap = sems(1)
+    hx, hk = x + w - 2 * x * w, k + c - 2 * k * c
+    z_dev, x_dev = partner((0, 1))[3], partner((1, 0))[3]
+
+    class Across:
+        def __init__(self, views):
+            self.views = views
+            self.n = len(views(x, k))
+            self.a, self.b = sems(3 * self.n)
+
+        def copies(self, leg):
+            refs = self.views(x, 1 - k) if leg == 2 else self.views(x, k)
+            at = self.n * leg
+            return [rc(v, v, self.a + at + i, self.b + at + i, z_dev if leg == 0 else x_dev) for i, v in enumerate(refs)]
+
+        def arrivals(self, leg):
+            refs = self.views(*((x, 1 - k), (1 - x, k), (1 - x, 1 - k))[leg])
+            at = self.n * leg
+            return [rc(v, v, self.a + at + i, self.b + at + i, z_dev if leg == 0 else x_dev) for i, v in enumerate(refs)]
+
+        def start(self):
+            begun(self)
+            self.passed = False
+            for leg in (0, 1):
+                for copy in self.copies(leg):
+                    copy.start()
+
+        def pass_on(self):
+            self.passed = True
+            for copy in self.arrivals(0):
+                copy.wait_recv()
+            for copy in self.copies(2):
+                copy.start()
+
+        def wait(self):
+            if not self.passed:
+                self.pass_on()
+            self.got = True
+            for leg in (1, 2):
+                for copy in self.arrivals(leg):
+                    copy.wait_recv()
+
+        def drain(self):
+            for leg in range(3):
+                for copy in self.copies(leg):
+                    copy.wait_send()
+
+    class Reduce:
+        def __init__(self, grad, rx, sz, rz):
+            self.grad, self.rx, self.sz, self.rz = grad, rx, sz, rz
+            self.runs = rx.shape[0]
+            self.a, self.b = sems(self.runs + 1)
+
+        def run(self, n):
+            return rc(self.grad.at[many(512 * n + 256 * (1 - x), 256)], self.rx.at[n], self.a + n, self.b + n, x_dev)
+
+        def last(self):
+            return rc(self.sz, self.rz, self.a + self.runs, self.b + self.runs, z_dev)
+
+        def start(self):
+            begun(self)
+            self.passed = False
+            for n in range(self.runs):
+                self.run(n).start()
+
+        def part(self, n, k_):
+            return (
+                self.grad[many(512 * n + 256 * x + 128 * k_, 128), :].astype(F32)
+                + self.rx[n, many(128 * k_, 128), :].astype(F32)
+            )
+
+        def pass_on(self):
+            self.passed = True
+            for n in range(self.runs):
+                self.run(n).wait_recv()
+            for n in range(self.runs):
+                self.sz[n] = self.part(n, 1 - k).astype(BF)
+            self.last().start()
+
+        def wait(self):
+            if not self.passed:
+                self.pass_on()
+            self.got = True
+            self.last().wait_recv()
+
+        def total(self, n):
+            return self.part(n, k) + self.rz[n].astype(F32)
+
+        def drain(self):
+            for n in range(self.runs):
+                self.run(n).wait_send()
+            self.last().wait_send()
+
     swap_rows = many(ROWS * (4 * k + 2 * w + c), ROWS)
-    swap_start(tokens, tok_all.at[swap_rows], *tok_swap)
+    tok_swap = Swap(tokens, tok_all.at[swap_rows])
+    cot_swap = Swap(cot, cot_all.at[swap_rows])
+    tok_swap.start()
+    raw[...] = jnp.zeros_like(raw)
+    raw[0:48, 0:32] = var_table[...].astype(F32)
+    for n, rows in ((48, norm_gain), (50, norm_shift), (52, qv_bias), (54, branch_bias)):
+        raw[n : n + 2, 0:32] = rows[...].astype(F32)
+    raw[56:57, 0:32] = lead_weight[...].astype(F32)
+    raw[64:65, :] = up_bias[...].astype(F32)
+    raw[65:66, 0:48] = var_mask[...].astype(F32)
+    raw[65:66, 64:65] = lead_hours[...].astype(F32)
+    packed = raw[0:16, :]
+    for t in range(1, 4):
+        packed = packed + pltpu.roll(raw[16 * t : 16 * t + 16, :], 32 * t, 1)
+    pack_in[0:16, :] = packed.astype(BF)
+    pack_in[16:32, :] = raw[64:80, :].astype(BF)
 
     own_rows = many(32 * idx, 32)
     copies = []
@@ -594,7 +749,6 @@
             copies.append((wup_in.at[:, many(128 * (16 * y_ + 8 * (r // 2) + 4 * (r % 2) + 2 * w_ + c_), 128)], wup.at[own_rows, pl.ds(128 * r, 128)], dv))
     in_up = Batch(copies)
     in_qkv.start()
-    cot_send = cot
 
     @pl.when(off_diag == 0)
     def _():
@@ -604,7 +758,7 @@
     for p in range(3):
         wqkv[own_rows, 128 * p : 128 * p + 128] = wqkv_in[:, many(128 * (8 * p + lane), 128)]
 
-    swap_wait(tokens, tok_all.at[swap_rows], *tok_swap)
+    tok_swap.wait()
     tok = Gather(tok_all)
     tok.start()
 
@@ -612,11 +766,14 @@
     place = 2 * w + c
     out_rows = many(32 * place, 32)
     home_dev = dev(y, x, k, x, k)
-    send_out = rc(wout_in, wout.at[out_rows], out_a, out_b + place, home_dev)
-
-    @pl.when(is_home == 0)
-    def _():
-        send_out.start()
+    pairs = ((0, 1), (1, 0), (1, 1))
+    away = 1 - is_home
+    out_in = []
+    for dw, dc in pairs:
+        m = 2 * flip(w, dw) + flip(c, dc)
+        out_in.append(rc(wout_in, wout.at[many(32 * m, 32)], out_a, out_b + m, home_dev))
+    to_home = Only(away, [rc(wout_in, wout.at[out_rows], out_a, out_b + place, home_dev)], is_home, out_in)
+    to_home.start()
 
     @pl.when(is_home == 1)
     def _():
@@ -624,50 +781,45 @@
 
     in_qkv.wait()
 
-    def between(pieces):
-        copies = []
-        for d in ranks:
-            x_, k_, r_, dv = partner(d)
-            for ref in pieces:
-                copies.append((ref, ref, dv))
-        return Batch(copies)
-
-    base = 16 * 0 + 8 * x + 4 * k
-    pack_pieces = [pack_all.at[pl.ds(base + 16 * y_, 4)] for y_ in range(2)]
-    qkv_pieces = [wqkv.at[many(512 * y_ + 256 * x + 128 * k, 128)] for y_ in range(2)]
-    up_pieces = [wup.at[many(512 * y_ + 256 * x + 128 * k, 128)] for y_ in range(2)]
+    def runs_of(ref, *more):
+        def views(x_, k_):
+            refs = [more[0].at[pl.ds(16 * y_ + 8 * x_ + 4 * k_, 4)] for y_ in range(2)] if more else []
+            return refs + [ref.at[many(512 * y_ + 256 * x_ + 128 * k_, 128)] for y_ in range(2)]
+
+        return views
+
     rank_rows = many(128 * rank, 128)
-    dp_qkv = between(pack_pieces + qkv_pieces)
+    dp_qkv = Across(runs_of(wqkv, pack_all))
+    dp_up = Across(runs_of(wup))
+    dp_down = Across(lambda x_, k_: [wdown.at[many(128 * (2 * x_ + k_), 128)]])
     dp_qkv.start()
+    cot_swap.start()
     in_up.start()
     for r in range(4):
         wup[own_rows, 128 * r : 128 * r + 128] = wup_in[:, many(128 * (16 * y + 8 * (r // 2) + 4 * (r % 2) + 2 * w + c), 128)]
     wdown[rank_rows, :] = wdown_in[...]
 
-    dpo_a, dpo_b = sems(3)
-    dp_out = [rc(wout, wout, dpo_a + n, dpo_b, partner(d)[3]) for n, d in enumerate(ranks)]
-
-    @pl.when(is_home == 1)
-    def _():
-        for dw, dc in ((0, 1), (1, 0), (1, 1)):
-            m = 2 * flip(w, dw) + flip(c, dc)
-            rows = many(32 * m, 32)
-            rc(wout_in, wout.at[rows], out_a, out_b + m, home_dev).wait_recv()
-        for copy in dp_out:
-            copy.start()
-
-    tok.pass_on()
-    swap_start(cot, cot_all.at[swap_rows], *cot_swap)
-
     @pl.when(off_diag == 0)
     def _():
         cot_all[my_rows, :] = cot[...]
 
+    dpo_a, dpo_b = sems(2)
+    out_z_copy = rc(wout, wout, dpo_a, dpo_b, z_dev)
+    out_x_copy = rc(wout, wout, dpo_a + 1, dpo_b + 1, x_dev)
+    dp_out = Only(is_home, [out_z_copy, out_x_copy], (1 - hx) * hk, [out_z_copy])
+    dp_out_more = Only((1 - hx) * hk, [out_x_copy], hx, [out_x_copy])
+    to_home.wait()
+    dp_out.start()
+    tok.pass_on()
     in_up.wait()
-    dp_up = between(up_pieces)
     dp_up.start()
-    dp_down = Batch([(wdown_in, wdown.at[rank_rows], partner(d)[3]) for d in ranks])
+    dp_qkv.pass_on()
+    dp_out.wait()
+    dp_out_more.start()
     dp_down.start()
+    cot_swap.wait()
+    cg = Gather(cot_all)
+    cg.start()
 
     dp_qkv.wait()
     lane_id = lax.broadcasted_iota(jnp.int32, (16, 128), 1)
@@ -675,29 +827,29 @@
         for t in range(4):
             block = None
             for m in range(4):
-                piece = pack_all[4 * b + m].astype(F32)
+                piece = pack_all[4 * b + m].astype(F32)[0:16, :]
                 shift = (32 * (m - t)) % 128
                 if shift:
                     piece = pltpu.roll(piece, shift, 1)
                 block = piece if block is None else jnp.where(lane_id // 32 == m, piece, block)
             full[16 * t : 16 * t + 16, 128 * b : 128 * b + 128] = block
 
-    gain0, gain1 = full[54:55, :], full[55:56, :]
-    shift0, shift1 = full[56:57, :], full[57:58, :]
+    gain0, gain1 = full[48:49, :], full[49:50, :]
+    shift0, shift1 = full[50:51, :], full[51:52, :]
     lane_cols = many(128 * lane, 128)
-    bias_q, bias_v = full[58:59, lane_cols], full[59:60, lane_cols]
-    bias_out, bias_down = full[60:61, :], full[61:62, :]
+    bias_q, bias_v = full[52:53, lane_cols], full[53:54, lane_cols]
+    bias_out, bias_down = full[54:55, :], full[55:56, :]
     bias_up = jnp.concatenate(
-        [pack_all[16 * y + 8 * (r // 2) + 4 * (r % 2) + 2 * w + c].astype(F32)[15:16, :] for r in range(4)], axis=1
-    )
-    facts = pack_all[8 * sample].astype(F32)[14:15, :]
+        [pack_all[16 * y + 8 * (r // 2) + 4 * (r % 2) + 2 * w + c].astype(F32)[16:17, :] for r in range(4)], axis=1
+    )
+    facts = pack_all[8 * sample].astype(F32)[17:18, :]
     one_lane = lax.broadcasted_iota(jnp.int32, (1, 128), 1)
     present = jnp.where(one_lane < 64, facts, 0.0)
     hours = jnp.sum(jnp.where(one_lane == 64, facts, 0.0), axis=-1, keepdims=True) * hours_scale
     present8 = jnp.broadcast_to(present, (8, 128))[:, :64].astype(BF)
-    extra = dot_nn(present8, full[...].astype(BF))[0:1, :] + hours * full[62:63, :]
-
-    tok.finish()
+    extra = dot_nn(present8, full[...].astype(BF))[0:1, :] + hours * full[56:57, :]
+
+    tok.wait()
 
     @pl.loop(0, 8)
     def _(n):
@@ -735,33 +887,30 @@
         attf[rows, :] = total
         att[rows, :] = total.astype(BF)
 
-    @pl.when(is_home == 0)
-    def _():
-        rc(wout, wout, dpo_a, dpo_b, home_dev).wait_recv()
+    dp_out_more.wait()
 
     def rows_of(l_):
         return many(ROWS * l_, ROWS)
 
+    cg.pass_on()
     rs_out = Scatter(0, lambda l_: dot_nn(att[rows_of(l_), :], wout[...]))
     rs_out.start()
 
-    swap_wait(cot, cot_all.at[swap_rows], *cot_swap)
-    cg = Gather(cot_all)
-    cg.start()
+    dp_up.pass_on()
+    dp_down.pass_on()
 
     stream = tok_all[my_rows, :].astype(F32) + extra
-    mid = stream + (rs_out.finish() + bias_out)
+    mid = stream + (rs_out.wait() + bias_out)
     middle[...] = mid
     xhat2, rstd2 = center(mid)
     n2_all[my_rows, :] = (xhat2 * gain1 + shift1).astype(BF)
     n2 = Gather(n2_all)
     n2.start()
-    cg.pass_on()
     n2.pass_on()
     dp_up.wait()
     dp_down.wait()
-    cg.finish()
-    n2.finish()
+    cg.wait()
+    n2.wait()
 
     upb_g[...] = jnp.zeros_like(upb_g)
 
@@ -778,10 +927,26 @@
 
     rs_n2 = Scatter(1, lambda l_: dot_nt(uplow[rows_of(l_), :], wup[...]))
     rs_n2.start()
-    rs_mix = Scatter(2, lambda l_: dot_nn(act[rows_of(l_), :], wdown[...]))
-    rs_mix.start()
-
-    n2_grad = rs_n2.finish()
+
+    @pl.loop(0, 4)
+    def _(r):
+        cols = many(128 * r, 128)
+        gdown[cols, :] = dot_tn(act[:, cols], cot_all[...]).astype(BF)
+
+    down_red = Reduce(gdown, xdown, zdown_s, zdown)
+    down_red.start()
+    upb_sends = Batch([(upb_g.at[:, many(128 * partner(d)[2], 128)], r_upb.at[n], partner(d)[3]) for n, d in enumerate(ranks)])
+    upb_sends.start()
+
+    @pl.loop(0, 4)
+    def _(n):
+        cols = many(256 * n, 256)
+        gup[cols, :] = dot_tn(n2_all[:, cols], uplow[...]).astype(BF)
+
+    up_red = Reduce(gup, xup, zup_s, zup)
+    up_red.start()
+
+    n2_grad = rs_n2.wait()
     incoming = cot_all[my_rows, :].astype(F32)
     xhat2, rstd2 = center(middle[...])
     mg = incoming + norm_back(xhat2, rstd2, gain1, n2_grad)
@@ -794,34 +959,12 @@
     smallp[5:6, :] = jnp.sum(mg.astype(BF).astype(F32), axis=0, keepdims=True)
     smallp[6:7, :] = jnp.sum(incoming, axis=0, keepdims=True)
 
-    @pl.loop(0, 4)
-    def _(r):
-        cols = many(128 * r, 128)
-        gdown[cols, :] = dot_tn(act[:, cols], cot_all[...]).astype(BF)
-
-    down_sends = Batch([(gdown.at[many(128 * partner(d)[2], 128)], rdown.at[n], partner(d)[3]) for n, d in enumerate(ranks)])
-    down_sends.start()
-    upb_sends_src = upb_g
-    upb_sends = Batch([(upb_g.at[:, many(128 * partner(d)[2], 128)], r_upb.at[n], partner(d)[3]) for n, d in enumerate(ranks)])
-    upb_sends.start()
+    down_red.pass_on()
     ml.pass_on()
-
-    @pl.loop(0, 4)
-    def _(n):
-        cols = many(256 * n, 256)
-        gup[cols, :] = dot_tn(n2_all[:, cols], uplow[...]).astype(BF)
-
-    def spread(src, recv):
-        copies = []
-        for n, d in enumerate(ranks):
-            x_, k_, r_, dv = partner(d)
-            for y_ in range(2):
-                copies.append((src.at[many(512 * y_ + 256 * x_ + 128 * k_, 128)], recv.at[n, pl.ds(128 * y_, 128)], dv))
-        return Batch(copies)
-
-    up_sends = spread(gup, rup)
-    up_sends.start()
-    ml.finish()
+    up_red.pass_on()
+    ml.wait()
+    rs_mix = Scatter(2, lambda l_: dot_nn(act[rows_of(l_), :], wdown[...]))
+    rs_mix.start()
 
     @pl.loop(0, 4)
     def _(n):
@@ -860,39 +1003,39 @@
         cols = many(256 * n, 256)
         gqkv[cols, :] = dot_tn(normed[:, cols], dproj[...]).astype(BF)
 
-    qkv_sends = spread(gqkv, rqkv)
-    qkv_sends.start()
-
-    n1_grad = rs_n1.finish()
+    qkv_red = Reduce(gqkv, xqkv, zqkv_s, zqkv)
+    qkv_red.start()
+    gout[...] = dot_tn(att[...], ml_all[...]).astype(BF)
+    go_a, go_b = sems(2)
+    grad_x = Only(hx, [rc(gout, out_x, go_a, go_b, x_dev)], 1 - hx, [rc(gout, out_x, go_a, go_b, x_dev)])
+    grad_z = Only((1 - hx) * hk, [rc(out_s, out_z, go_a + 1, go_b + 1, z_dev)], is_home, [rc(out_s, out_z, go_a + 1, go_b + 1, z_dev)])
+    grad_x.start()
+    mixed_low = (middle[...] + (rs_mix.wait() + bias_down)).astype(BF)
+    tgr[2] = mixed_low
+    mix_swap = Swap(tgr.at[2], tgr.at[3])
+    mix_swap.start()
+    qkv_red.pass_on()
+    grad_x.wait()
+
+    @pl.when(hx == 0)
+    def _():
+        out_s[...] = (gout[...].astype(F32) + out_x[...].astype(F32)).astype(BF)
+
+    grad_z.start()
+
+    n1_grad = rs_n1.wait()
     xhat1, rstd1 = center(tok_all[my_rows, :].astype(F32) + extra)
     tg = mgrad[...] + norm_back(xhat1, rstd1, gain0, n1_grad)
-    tgs[...] = tg
-    tg_swap = sems(1)
-    tgs_b = tgr.at[0]
     tgr[0] = tg.astype(BF)
-    swap_start(tgr.at[0], tgr.at[1], *tg_swap)
+    tg_swap = Swap(tgr.at[0], tgr.at[1])
+    tg_swap.start()
     smallp[0:1, :] = jnp.sum(tg, axis=0, keepdims=True)
     smallp[1:2, :] = jnp.sum(n1_grad * xhat1, axis=0, keepdims=True)
     smallp[3:4, :] = jnp.sum(n1_grad, axis=0, keepdims=True)
     smallp[7:8, :] = jnp.zeros((1, D), F32)
 
-    gout[...] = dot_tn(att[...], ml_all[...]).astype(BF)
-    go_a, go_b = sems(4)
-    hx, hk = x + w - 2 * x * w, k + c - 2 * k * c
-    apart = 2 * hx + hk
-    send_home = rc(gout, rout.at[apart], go_a, go_b + apart, dev(y, w, c, w, c))
-
-    @pl.when(is_home == 0)
-    def _():
-        send_home.start()
-
     small_group = Batch([(smallp.at[:, many(128 * peer(d)[3], 128)], r_a.at[n], peer(d)[4]) for n, d in enumerate(group)])
     small_group.start()
-
-    mix_swap = sems(1)
-    mixed_low = (middle[...] + (rs_mix.finish() + bias_down)).astype(BF)
-    tgr[2] = mixed_low
-    swap_start(tgr.at[2], tgr.at[3], *mix_swap)
 
     small_group.wait()
     total = smallp[:, lane_cols]
@@ -906,19 +1049,8 @@
     small_ranks = Batch([(s_b, r_b.at[n], partner(d)[3]) for n, d in enumerate(ranks)])
     small_ranks.start()
 
-    down_sends.wait()
-    sum_down = gdown[rank_rows, :].astype(F32)
-    for n in range(3):
-        sum_down = sum_down + rdown[n].astype(F32)
-    gd_o[...] = sum_down
-    mine = [many(512 * y_ + 256 * x + 128 * k, 128) for y_ in range(2)]
-
-    def collect(src, recv, low_sum):
-        for y_ in range(2):
-            part = src[mine[y_], :].astype(F32)
-            for n in range(3):
-                part = part + recv[n, 128 * y_ : 128 * y_ + 128, :].astype(F32)
-            low_sum[128 * y_ : 128 * y_ + 128, :] = part.astype(BF)
+    down_red.wait()
+    gd_o[...] = down_red.total(0).astype(BF)
 
     def deal(low_sum, recv):
         copies = []
@@ -927,47 +1059,38 @@
             copies.append((low_sum.at[many(128 * y_ + 64 * w_ + 32 * c_, 32)], recv.at[lane], dv))
         return Batch(copies)
 
-    my_deal = many(128 * y + 64 * w + 32 * c, 32)
-    up_sends.wait()
-    collect(gup, rup, su2)
-    up_deal = deal(su2, ru2)
-    up_deal.start()
-    ru2[lane] = su2[my_deal, :]
+    def collect(red, low_sum, recv):
+        red.wait()
+        for y_ in range(2):
+            low_sum[128 * y_ : 128 * y_ + 128, :] = red.total(y_).astype(BF)
+        batch = deal(low_sum, recv)
+        batch.start()
+        recv[lane] = low_sum[many(128 * y + 64 * w + 32 * c, 32), :]
+        return batch
+
+    up_deal = collect(up_red, su2, ru2)
+    grad_z.wait()
 
     @pl.when(is_home == 1)
     def _():
-        for n, d in enumerate(ranks):
-            slot = 2 * d[0] + d[1]
-            rc(gout, rout.at[slot], go_a, go_b + slot, partner(d)[3]).wait_recv()
-        sum_out = gout[...].astype(F32)
-        for slot in range(1, 4):
-            sum_out = sum_out + rout[slot].astype(F32)
-        so2[...] = sum_out.astype(BF)
+        so2[...] = (out_s[...].astype(F32) + out_z[...].astype(F32)).astype(BF)
+        go_o[...] = so2[out_rows, :]
 
     outs_a, outs_b = sems(3)
-    home_copies = []
-    for n, (dw, dc) in enumerate(((0, 1), (1, 0), (1, 1))):
+    copies = []
+    for n, (dw, dc) in enumerate(pairs):
         w_, c_ = flip(w, dw), flip(c, dc)
-        home_copies.append(rc(so2.at[many(32 * (2 * w_ + c_), 32)], ro2, outs_a + n, outs_b, dev(y, x, k, w_, c_)))
-
-    @pl.when(is_home == 1)
-    def _():
-        for copy in home_copies:
-            copy.start()
-        go_o[...] = so2[out_rows, :].astype(F32)
-
-    qkv_sends.wait()
-    collect(gqkv, rqkv, sq2)
-    qkv_deal = deal(sq2, rq2)
-    qkv_deal.start()
-    rq2[lane] = sq2[my_deal, :]
+        copies.append(rc(so2.at[many(32 * (2 * w_ + c_), 32)], ro2, outs_a + n, outs_b, dev(y, x, k, w_, c_)))
+    out_deal = Only(is_home, copies, away, [rc(so2.at[pl.ds(0, 32)], ro2, outs_a, outs_b, home_dev)])
+    out_deal.start()
+    qkv_deal = collect(qkv_red, sq2, rq2)
 
     small_ranks.wait()
     blocks = [None] * 4
     rows_sum = s_b[...]
     for n in range(3):
         rows_sum = rows_sum + r_b[n]
-    own_facts = [facts] + [pack_all[8 * (2 * partner(d)[1] + partner(d)[0])].astype(F32)[14:15, :] for d in ranks]
+    own_facts = [facts] + [pack_all[8 * (2 * partner(d)[1] + partner(d)[0])].astype(F32)[17:18, :] for d in ranks]
     own_sums = [s_b[0:1, :]] + [r_b[n, 0:1, :] for n in range(3)]
     facts8 = jnp.concatenate(own_facts + [jnp.zeros((4, 128), F32)], axis=0)
     facts_t = jnp.transpose(facts8)
@@ -980,20 +1103,20 @@
     s_a[80:81, :] = table[64:65, :] * hours_scale
     s_a[81:88, :] = jnp.zeros((7, 128), F32)
     sm_a, sm_b = sems(3)
-    small_copies = []
-    for n, (dw, dc) in enumerate(((0, 1), (1, 0), (1, 1))):
+    copies = []
+    for n, (dw, dc) in enumerate(pairs):
         w_, c_ = flip(w, dw), flip(c, dc)
-        small_copies.append(rc(s_a, r_c, sm_a + n, sm_b, dev(y, x, k, w_, c_)))
+        copies.append(rc(s_a, r_c, sm_a + n, sm_b, dev(y, x, k, w_, c_)))
+    small_deal = Only(is_home, copies, away, [rc(s_a, r_c, sm_a, sm_b, home_dev)])
+    small_deal.start()
+    small_deal.wait()
 
     @pl.when(is_home == 1)
     def _():
-        for copy in small_copies:
-            copy.start()
         small_o[0:88, :] = s_a[...]
 
     @pl.when(is_home == 0)
     def _():
-        rc(s_a, r_c, sm_a, sm_b, home_dev).wait_recv()
         small_o[0:88, :] = r_c[...]
 
     upb_sends.wait()
@@ -1002,110 +1125,116 @@
         sum_upb = sum_upb + r_upb[n]
     small_o[88:96, :] = sum_upb
 
+    out_deal.wait()
+
     @pl.when(is_home == 0)
     def _():
-        rc(so2.at[pl.ds(0, 32)], ro2, outs_a, outs_b, home_dev).wait_recv()
-        go_o[...] = ro2[...].astype(F32)
+        go_o[...] = ro2[...]
 
     @pl.when(off_diag == 0)
     def _():
-        tg_o[...] = tgs[...]
+        tg_o[...] = tgr[0]
         mixed_o[...] = tgr[2]
 
-    swap_wait(tgr.at[2], tgr.at[3], *mix_swap)
-    swap_wait(tgr.at[0], tgr.at[1], *tg_swap)
+    mix_swap.wait()
+    tg_swap.wait()
 
     @pl.when(off_diag == 1)
     def _():
-        tg_o[...] = tgr[1].astype(F32)
+        tg_o[...] = tgr[1]
         mixed_o[...] = tgr[3]
 
     up_deal.wait()
+    gu_o[...] = ru2[...]
+    qkv_deal.wait()
+    gq_o[...] = rq2[...]
+
+    finish_all()
+
+
+def finish_kernel(
+    mixed_i, tg_i, gq_i, go_i, gu_i, gd_i, small_i,
+    mixed_o, tg_o, table_o, lead_o, gain_o, shift_o, gq_o, qv_o, go_o, bias_o, gu_o, upb_o, gd_o,
+):
+    mixed_o[0] = mixed_i[...]
+    tg_o[0] = tg_i[...].astype(F32)
+    gd_o[...] = gd_i[...].astype(F32)
+    go_o[...] = go_i[...].astype(F32)
     for l_ in range(8):
-        part = ru2[l_].astype(F32)
+        part = gu_i[l_].astype(F32)
         y_, w_, c_ = l_ // 4, (l_ // 2) % 2, l_ % 2
         for r in range(4):
             at = 128 * (16 * y_ + 8 * (r // 2) + 4 * (r % 2) + 2 * w_ + c_)
             gu_o[:, at : at + 128] = part[:, 128 * r : 128 * r + 128]
-    qkv_deal.wait()
-    for l_ in range(8):
-        part = rq2[l_].astype(F32)
+        part = gq_i[l_].astype(F32)
         for p in range(3):
             at = 128 * (8 * p + l_)
             gq_o[:, at : at + 128] = part[:, 128 * p : 128 * p + 128]
-
-    for item in (in_qkv, in_up, dp_qkv, dp_up, dp_down, tok, cg, n2, ml, rs_out, rs_n2, rs_mix, rs_n1,
-                 down_sends, upb_sends, up_sends, qkv_sends, small_group, small_ranks, up_deal, qkv_deal):
-        item.drain()
-
-    @pl.when(is_home == 0)
-    def _():
-        send_out.wait_send()
-        send_home.wait_send()
-
-    @pl.when(is_home == 1)
-    def _():
-        for copy in dp_out + home_copies + small_copies:
-            copy.wait_send()
+    place = lax.rem(lax.axis_index("seq"), 4)
+    small = small_i[0:88, :]
+    mine = small
+    for m in range(1, 4):
+        mine = jnp.where(place == m, pltpu.roll(small, 128 - 32 * m, 1), mine)
+    table_o[...] = mine[0:48, 0:32]
+    gain_o[...] = mine[65:67, 0:32]
+    shift_o[...] = mine[67:69, 0:32]
+    bias_o[...] = mine[69:71, 0:32]
+    qv_o[...] = mine[72:74, 0:32]
+    lead_o[...] = mine[80:81, 0:32]
+    upb_o[...] = small_i[88:89, :]
 
 
 def local_fast(
     tokens, lead_hours, var_mask, var_table, lead_weight, norm_gain, norm_shift, w_qkv, qv_bias, w_out,
     branch_bias, w_up, up_bias, w_down, cotangent,
 ):
-    mask = var_mask.astype(BF)[0]
-    zero = jnp.zeros((1, 2), BF)
-    parts = [mask[14 * t : min(14 * t + 14, 48)] for t in range(4)]
-    slots = jnp.concatenate([parts[0], zero[0], parts[1], zero[0], parts[2], zero[0], parts[3], jnp.zeros((10,), BF)])
-    hours = jnp.concatenate([lead_hours.astype(BF), jnp.zeros((31,), BF)])
-    ub = up_bias.reshape(4, 32)
-    rows = jnp.concatenate(
-        [
-            var_table[0:14], slots[None, 0:32], ub[0:1],
-            var_table[14:28], slots[None, 32:64], ub[1:2],
-            var_table[28:42], hours[None], ub[2:3],
-            var_table[42:48], norm_gain, norm_shift, qv_bias, branch_bias, lead_weight[None], ub[3:4],
-        ],
-        axis=0,
-    )
-    pack = rows.reshape(4, 16, 32).transpose(1, 0, 2).reshape(16, 128)
-
     vm = pltpu.VMEM
     scratch = [
         vm((D, D), BF), vm((D, D), BF), vm((D, D), BF), vm((D, D), BF),
-        vm((D, 384), BF), vm((D, FFL), BF), vm((FFL, D), BF), vm((128, D), BF), vm((32, 16, 128), BF), vm((64, D), F32),
+        vm((D, 384), BF), vm((D, FFL), BF), vm((FFL, D), BF), vm((128, D), BF), vm((80, 128), F32), vm((32, 128), BF), vm((32, 32, 128), BF), vm((64, D), F32),
         vm((D, D), BF), vm((D, 128), BF), vm((D, 128), BF), vm((D, 128), BF), vm((2, D, D), BF), vm((D, 128), F32), vm((D, 128), BF),
         vm((4, 4, 128, D), BF), vm((4, 4, 128, D), BF), vm((4, 3, 128, D), BF), vm((4, 3, 128, D), BF), vm((4, 128, D), F32),
         vm((128, D), F32), vm((128, D), F32), vm((D, FFL), BF), vm((D, FFL), BF), vm((D, 384), BF), vm((D, 128), BF), vm((D, 128), F32), vm((D, 128), F32),
         vm((D, 384), BF), vm((D, FFL), BF), vm((FFL, D), BF), vm((128, D), BF),
-        vm((3, 256, 384), BF), vm((3, 256, FFL), BF), vm((3, 128, D), BF), vm((4, 128, D), BF),
+        vm((2, 256, 384), BF), vm((2, 256, FFL), BF), vm((1, 256, D), BF),
+        vm((2, 128, 384), BF), vm((2, 128, FFL), BF), vm((1, 128, D), BF),
+        vm((2, 128, 384), BF), vm((2, 128, FFL), BF), vm((1, 128, D), BF),
+        vm((128, D), BF), vm((128, D), BF), vm((128, D), BF),
         vm((256, 384), BF), vm((256, FFL), BF), vm((8, 32, 384), BF), vm((8, 32, FFL), BF), vm((128, D), BF), vm((32, D), BF),
-        vm((128, D), F32), vm((4, 128, D), BF), vm((8, D), F32), vm((88, 128), F32), vm((7, 8, 128), F32), vm((16, 128), F32), vm((3, 16, 128), F32), vm((88, 128), F32),
+        vm((4, 128, D), BF), vm((8, D), F32), vm((88, 128), F32), vm((7, 8, 128), F32), vm((16, 128), F32), vm((3, 16, 128), F32), vm((88, 128), F32),
         vm((8, FFL), F32), vm((3, 8, 128), F32),
         pltpu.SemaphoreType.DMA((260,)), pltpu.SemaphoreType.DMA((260,)),
     ]
-    outs = [
-        jax.ShapeDtypeStruct((128, D), BF), jax.ShapeDtypeStruct((128, D), F32), jax.ShapeDtypeStruct((32, 3 * D), F32),
-        jax.ShapeDtypeStruct((32, D), F32), jax.ShapeDtypeStruct((32, 4 * D), F32), jax.ShapeDtypeStruct((128, D), F32),
-        jax.ShapeDtypeStruct((96, 128), F32),
-    ]
-    mixed, tg, gq, go, gu, gd, small = pl.pallas_call(
+    shape = jax.ShapeDtypeStruct
+    raw = pl.pallas_call(
         fast_kernel,
-        out_shape=outs,
-        in_specs=[pl.BlockSpec(memory_space=vm)] * 7,
+        out_shape=[
+            shape((128, D), BF), shape((128, D), BF), shape((8, 32, 384), BF), shape((32, D), BF), shape((8, 32, FFL), BF),
+            shape((128, D), BF), shape((96, 128), F32),
+        ],
+        in_specs=[pl.BlockSpec(memory_space=vm)] * 15,
         out_specs=[pl.BlockSpec(memory_space=vm)] * 7,
         scratch_shapes=scratch,
         compiler_params=pltpu.CompilerParams(collective_id=0, has_side_effects=True, vmem_limit_bytes=62 * 2**20),
         cost_estimate=pl.CostEstimate(flops=14_000_000_000, bytes_accessed=4_000_000, transcendentals=6_000_000),
-    )(tokens[0], cotangent[0], w_qkv, w_out, w_up, w_down, pack)
-    place = lax.axis_index("seq") % 4
-    mine = lax.dynamic_slice(small, (0, 32 * place), (88, 32))
-    table = jnp.concatenate([mine[0:14], mine[16:30], mine[32:46], mine[48:54]], axis=0)
-    tail = mine[64:80]
-    return (
-        mixed[None], tg[None], table, mine[80],
-        tail[1:3], tail[3:5], gq, tail[8:10], go, tail[5:7], gu, small[88], gd,
-    )
+    )(
+        tokens[0], lead_hours[None], var_mask, var_table, lead_weight[None], norm_gain, norm_shift, w_qkv, qv_bias, w_out,
+        branch_bias, w_up, up_bias[None], w_down, cotangent[0],
+    )
+    out = pl.pallas_call(
+        finish_kernel,
+        out_shape=[
+            shape((1, 128, D), BF), shape((1, 128, D), F32), shape((48, 32), F32), shape((1, 32), F32), shape((2, 32), F32),
+            shape((2, 32), F32), shape((32, 3 * D), F32), shape((2, 32), F32), shape((32, D), F32), shape((2, 32), F32),
+            shape((32, 4 * D), F32), shape((1, 128), F32), shape((128, D), F32),
+        ],
+        in_specs=[pl.BlockSpec(memory_space=vm)] * 7,
+        out_specs=[pl.BlockSpec(memory_space=vm)] * 13,
+        compiler_params=pltpu.CompilerParams(vmem_limit_bytes=32 * 2**20),
+        cost_estimate=pl.CostEstimate(flops=1_000_000, bytes_accessed=4_000_000, transcendentals=0),
+    )(*raw)
+    mixed, tg, table, lead, gain, shift, gq, qv, go, bias, gu, upb, gd = out
+    return (mixed, tg, table, lead[0], gain, shift, gq, qv, go, bias, gu, upb[0], gd)
 
 
 def solution(mesh):

time: 280 us -> 222 us (0.79)
  Pallas kernels: 261 us -> 212 us
  local copies, waits for them, and re-layouts: 16.3 us -> 7.75 us
    pallas_call x1 -> x2, Pallas kernels: 261 us -> 212 us  [the longest x1 211 us: local_fast(): pl.pallas_call(fast_kernel, out_shape=[shape((128, D), BF), shape((128, D...]
    slice x8 -> x0, local copies, waits for them, and re-layouts: 3.47 us -> none  [the longest x1 1.44 us: local_fast(): tail[5:7]]
    unnamed x37 -> x18, local copies, waits for them, and re-layouts: 9.5 us -> 7.75 us
where the time goes in v2:
time: 222 us
  Pallas kernels  212 us (95%)
  local copies, waits for them, and re-layouts  7.75 us (3%)
    pallas_call x1, Pallas kernels, local_fast(): pl.pallas_call(fast_kernel, out_shape=[shape((128, D), BF), shape((128, D...  211 us
    unnamed x18, local copies, waits for them, and re-layouts  7.75 us

profile of v2, /device:TPU:0, one launch (start us, length us, event | category | flops | bytes accessed | tf_op | source)
XLA Modules:
  0.0 221.5 jit_solution(16924223081235605830)
XLA Ops:
  0.6 0.0 copy-start.7
  1.3 0.0 copy-done.7
  1.3 0.7 copy.28.var_table
  2.0 211.0 %shard_map.246 = (bf16[128,1024]{1,0:T(8,128)(2,1)}, bf16[128,1024]{1,0:T(8,128)(2,1)}, bf16[8,32,384]{2,1,0:T(8,128)(2,1)}, bf16[32,1024]{1,0:T(8,128)(2,1)}, b...) custom-call(bf16[128,1024]{1,0:T(8,128)(2,1)} %bitcast.8, s32[1,1]{1,0:T(1,128)} %bitcast.7.lead_hours, ...), custom_call_target="tpu_custom_call" | custom-call | flops 14000000000 | bytes 4000000 | tf_op jit(solution)/shard_map/pallas_call | solution.py:1209
  213.0 0.0 copy-start
  213.0 0.9 copy-done
  214.0 0.0 copy-start.1
  214.0 0.9 copy-done.1
  214.9 0.0 copy-start.2
  214.9 0.9 copy-done.2
  215.9 0.0 copy-start.3
  215.9 0.9 copy-done.3
  216.8 0.0 copy-start.4
  216.8 0.9 copy-done.4
  217.8 0.0 copy-start.5
  217.8 0.8 copy-done.5
  218.6 0.0 copy-start.6
  218.6 0.8 copy-done.6
  219.4 1.5 shard_map.247
  220.9 0.7 copy.29
Async XLA Ops:
  0.6 0.7 copy-start.7
  213.0 1.0 copy-start
  214.0 0.9 copy-start.1
  214.9 0.9 copy-start.2
  215.9 0.9 copy-start.3
  216.8 0.9 copy-start.4
  217.8 0.8 copy-start.5
  218.6 0.8 copy-start.6

commit v3 on v2

--- a/solution.py
+++ b/solution.py
@@ -383,18 +383,18 @@
 
 
 def fast_kernel(
-    tokens, lead_hours, var_mask, var_table, lead_weight, norm_gain, norm_shift, wqkv_in, qv_bias, wout_in,
-    branch_bias, wup_in, up_bias, wdown_in, cot,
+    tokens_h, lead_hours, var_mask, var_table, lead_weight, norm_gain, norm_shift, wqkv_h, qv_bias, wout_h,
+    branch_bias, wup_h, up_bias, wdown_h, cot_h,
     mixed_o, tg_o, gq_o, go_o, gu_o, gd_o, small_o,
-    tok_all, cot_all, n2_all, ml_all,
+    tokens, wqkv_in, wup_in, wout_in, cot, tok_all, cot_all, n2_all, ml_all,
     wqkv, wup, wdown, wout, raw, pack_in, pack_all, full,
     normed, q_s, k_s, v_s, shares, attf, att,
-    rs_s1, rs_r1, rs_s2, rs_r2, own,
+    rs_s1, rs_r1, rs_s2, rs_r2, own, kept,
     middle, mgrad, act, uplow, dproj, dog, dk_acc, dv_acc,
     gqkv, gup, gdown, gout, xqkv, xup, xdown, zqkv_s, zup_s, zdown_s, zqkv, zup, zdown,
     out_x, out_s, out_z, sq2, su2, rq2, ru2, so2, ro2,
-    tgr, smallp, s_a, r_a, s_b, r_b, r_c, upb_g, r_upb,
-    ss, rs,
+    tgr, smallp, r_a, s_b, r_b, upb_g, r_upb,
+    ss, rs, ls,
 ):
     s_i = lax.axis_index("samp")
     q_i = lax.axis_index("seq")
@@ -440,6 +440,7 @@
 
     swap_dev = dev(k, x, y, w, c)
 
+    rank_rows = many(128 * rank, 128)
     barrier = pltpu.get_barrier_semaphore()
     for d in group:
         pl.semaphore_signal(barrier, inc=1, device_id=peer(d)[4], device_id_type=MESH)
@@ -450,276 +451,12 @@
     def _():
         pl.semaphore_signal(barrier, inc=1, device_id=swap_dev, device_id_type=MESH)
 
-    pl.semaphore_wait(barrier, 10 + off_diag)
-
-    def begun(item):
-        items.append(item)
-        item.got = False
-
-    class Swap:
-        def __init__(self, src, dst):
-            self.copy = rc(src, dst, *sems(1), swap_dev)
-
-        def start(self):
-            begun(self)
-            pl.when(off_diag == 1)(self.copy.start)
-
-        def wait(self):
-            self.got = True
-            pl.when(off_diag == 1)(self.copy.wait_recv)
-
-        def drain(self):
-            pl.when(off_diag == 1)(self.copy.wait_send)
-
-    class Only:
-        def __init__(self, sends, outgoing, takes, incoming):
-            self.sends, self.outgoing, self.takes, self.incoming = sends, outgoing, takes, incoming
-
-        def each(self, flag, copies, name):
-            @pl.when(flag == 1)
-            def _():
-                for copy in copies:
-                    getattr(copy, name)()
-
-        def start(self):
-            begun(self)
-            self.each(self.sends, self.outgoing, "start")
-
-        def wait(self):
-            self.got = True
-            self.each(self.takes, self.incoming, "wait_recv")
-
-        def drain(self):
-            self.each(self.sends, self.outgoing, "wait_send")
-
-    def finish_all():
-        for item in items:
-            if not item.got:
-                item.wait()
-        for item in items:
-            item.drain()
-
-    class Gather:
-        def __init__(self, buf):
-            self.buf = buf
-            self.a, self.b = sems(8)
-
-        def copy(self, i, forward):
-            dy, dw = chips[i]
-            if i == 0:
-                return rc(self.buf.at[my_rows], self.buf.at[my_rows], self.a, self.b, peer((0, 0, 1))[4])
-            y_, w_, c_, l_, dv = peer((dy, dw, 0))
-            if forward:
-                rows = many(ROWS * l_, ROWS)
-                return rc(self.buf.at[rows], self.buf.at[rows], self.a + 4 + i, self.b + 4 + i, peer((0, 0, 1))[4])
-            return rc(self.buf.at[my_rows], self.buf.at[my_rows], self.a + i, self.b + i, dv)
-
-        def start(self):
-            begun(self)
-            self.passed = False
-            for i in (3, 1, 2, 0):
-                self.copy(i, False).start()
-
-        def pass_on(self):
-            self.passed = True
-            for i in (1, 2, 3):
-                self.copy(i, False).wait_recv()
-                self.copy(i, True).start()
-
-        def wait(self):
-            if not self.passed:
-                self.pass_on()
-            self.got = True
-            self.copy(0, False).wait_recv()
-            for i in (1, 2, 3):
-                self.copy(i, True).wait_recv()
-
-        def drain(self):
-            for i in range(4):
-                self.copy(i, False).wait_send()
-            for i in (1, 2, 3):
-                self.copy(i, True).wait_send()
-
-    class Scatter:
-        def __init__(self, slot, partial):
-            self.slot = slot
-            self.partial = partial
-            self.a1, self.b1 = sems(4)
-            self.a2, self.b2 = sems(4)
-
-        def far(self, i):
-            dy, dw = i // 2, i % 2
-            y_, w_ = y + dy - 2 * y * dy, w + dw - 2 * w * dw
-            return y_, w_
-
-        def first(self, i):
-            return rc(rs_s1.at[self.slot, i], rs_r1.at[self.slot, i], self.a1 + i, self.b1 + i, dev(y, x, k, w, 1 - c))
-
-        def second(self, i):
-            y_, w_ = self.far(i)
-            return rc(rs_s2.at[self.slot, i - 1], rs_r2.at[self.slot, i - 1], self.a2 + i, self.b2 + i, dev(y_, x, k, w_, c))
-
-        def start(self):
-            begun(self)
-
-            @pl.loop(0, 4)
-            def _(n):
-                i = 3 - n
-                y_, w_ = self.far(i)
-                rs_s1[self.slot, i] = self.partial(4 * y_ + 2 * w_ + 1 - c).astype(BF)
-                self.first(i).start()
-
-            @pl.loop(0, 4)
-            def _(n):
-                i = 3 - n
-                y_, w_ = self.far(i)
-                part = self.partial(4 * y_ + 2 * w_ + c)
-                self.first(i).wait_recv()
-                total = part + rs_r1[self.slot, i].astype(F32)
-
-                @pl.when(i > 0)
-                def _():
-                    rs_s2[self.slot, i - 1] = total.astype(BF)
-                    self.second(i).start()
-
-                @pl.when(i == 0)
-                def _():
-                    own[self.slot] = total
-
-        def wait(self):
-            self.got = True
-            for i in (1, 2, 3):
-                self.second(i).wait_recv()
-            total = own[self.slot]
-            for i in (1, 2, 3):
-                total = total + rs_r2[self.slot, i - 1].astype(F32)
-            return total
-
-        def drain(self):
-            for i in range(4):
-                self.first(i).wait_send()
-            for i in (1, 2, 3):
-                self.second(i).wait_send()
-
-    class Batch:
-        def __init__(self, copies):
-            self.copies = copies
-            self.a, self.b = sems(len(copies))
-
-        def copy(self, n):
-            src, dst, device = self.copies[n]
-            return rc(src, dst, self.a + n, self.b + n, device)
-
-        def start(self):
-            begun(self)
-            for n in range(len(self.copies)):
-                self.copy(n).start()
-
-        def wait(self):
-            self.got = True
-            for n in range(len(self.copies)):
-                self.copy(n).wait_recv()
-
-        def drain(self):
-            for n in range(len(self.copies)):
-                self.copy(n).wait_send()
-
-    hx, hk = x + w - 2 * x * w, k + c - 2 * k * c
-    z_dev, x_dev = partner((0, 1))[3], partner((1, 0))[3]
-
-    class Across:
-        def __init__(self, views):
-            self.views = views
-            self.n = len(views(x, k))
-            self.a, self.b = sems(3 * self.n)
-
-        def copies(self, leg):
-            refs = self.views(x, 1 - k) if leg == 2 else self.views(x, k)
-            at = self.n * leg
-            return [rc(v, v, self.a + at + i, self.b + at + i, z_dev if leg == 0 else x_dev) for i, v in enumerate(refs)]
-
-        def arrivals(self, leg):
-            refs = self.views(*((x, 1 - k), (1 - x, k), (1 - x, 1 - k))[leg])
-            at = self.n * leg
-            return [rc(v, v, self.a + at + i, self.b + at + i, z_dev if leg == 0 else x_dev) for i, v in enumerate(refs)]
-
-        def start(self):
-            begun(self)
-            self.passed = False
-            for leg in (0, 1):
-                for copy in self.copies(leg):
-                    copy.start()
-
-        def pass_on(self):
-            self.passed = True
-            for copy in self.arrivals(0):
-                copy.wait_recv()
-            for copy in self.copies(2):
-                copy.start()
-
-        def wait(self):
-            if not self.passed:
-                self.pass_on()
-            self.got = True
-            for leg in (1, 2):
-                for copy in self.arrivals(leg):
-                    copy.wait_recv()
-
-        def drain(self):
-            for leg in range(3):
-                for copy in self.copies(leg):
-                    copy.wait_send()
-
-    class Reduce:
-        def __init__(self, grad, rx, sz, rz):
-            self.grad, self.rx, self.sz, self.rz = grad, rx, sz, rz
-            self.runs = rx.shape[0]
-            self.a, self.b = sems(self.runs + 1)
-
-        def run(self, n):
-            return rc(self.grad.at[many(512 * n + 256 * (1 - x), 256)], self.rx.at[n], self.a + n, self.b + n, x_dev)
-
-        def last(self):
-            return rc(self.sz, self.rz, self.a + self.runs, self.b + self.runs, z_dev)
-
-        def start(self):
-            begun(self)
-            self.passed = False
-            for n in range(self.runs):
-                self.run(n).start()
-
-        def part(self, n, k_):
-            return (
-                self.grad[many(512 * n + 256 * x + 128 * k_, 128), :].astype(F32)
-                + self.rx[n, many(128 * k_, 128), :].astype(F32)
-            )
-
-        def pass_on(self):
-            self.passed = True
-            for n in range(self.runs):
-                self.run(n).wait_recv()
-            for n in range(self.runs):
-                self.sz[n] = self.part(n, 1 - k).astype(BF)
-            self.last().start()
-
-        def wait(self):
-            if not self.passed:
-                self.pass_on()
-            self.got = True
-            self.last().wait_recv()
-
-        def total(self, n):
-            return self.part(n, k) + self.rz[n].astype(F32)
-
-        def drain(self):
-            for n in range(self.runs):
-                self.run(n).wait_send()
-            self.last().wait_send()
-
-    swap_rows = many(ROWS * (4 * k + 2 * w + c), ROWS)
-    tok_swap = Swap(tokens, tok_all.at[swap_rows])
-    cot_swap = Swap(cot, cot_all.at[swap_rows])
-    tok_swap.start()
+    loads = [
+        pltpu.make_async_copy(src, dst, ls.at[n])
+        for n, (src, dst) in enumerate(((tokens_h, tokens), (wqkv_h, wqkv_in), (wup_h, wup_in), (wout_h, wout_in), (cot_h, cot), (wdown_h, wdown.at[rank_rows])))
+    ]
+    for load in loads:
+        load.start()
     raw[...] = jnp.zeros_like(raw)
     raw[0:48, 0:32] = var_table[...].astype(F32)
     for n, rows in ((48, norm_gain), (50, norm_shift), (52, qv_bias), (54, branch_bias)):
@@ -733,8 +470,309 @@
         packed = packed + pltpu.roll(raw[16 * t : 16 * t + 16, :], 32 * t, 1)
     pack_in[0:16, :] = packed.astype(BF)
     pack_in[16:32, :] = raw[64:80, :].astype(BF)
-
+    for load in loads[:4]:
+        load.wait()
+    pl.semaphore_wait(barrier, 10 + off_diag)
+
+    def begun(item):
+        items.append(item)
+        item.got = False
+
+    class Swap:
+        def __init__(self, src, dst):
+            self.copy = rc(src, dst, *sems(1), swap_dev)
+
+        def start(self):
+            begun(self)
+            pl.when(off_diag == 1)(self.copy.start)
+
+        def wait(self):
+            self.got = True
+            pl.when(off_diag == 1)(self.copy.wait_recv)
+
+        def drain(self):
+            pl.when(off_diag == 1)(self.copy.wait_send)
+
+    class Only:
+        def __init__(self, sends, outgoing, takes, incoming):
+            self.sends, self.outgoing, self.takes, self.incoming = sends, outgoing, takes, incoming
+
+        def each(self, flag, copies, name):
+            @pl.when(flag == 1)
+            def _():
+                for copy in copies:
+                    getattr(copy, name)()
+
+        def start(self):
+            begun(self)
+            self.each(self.sends, self.outgoing, "start")
+
+        def wait(self):
+            self.got = True
+            self.each(self.takes, self.incoming, "wait_recv")
+
+        def drain(self):
+            self.each(self.sends, self.outgoing, "wait_send")
+
+    def finish_all():
+        for item in items:
+            if not item.got:
+                item.wait()
+        for item in items:
+            item.drain()
+
+    y_nbr, w_nbr, sibling = dev(1 - y, x, k, w, c), dev(y, x, k, 1 - w, c), dev(y, x, k, w, 1 - c)
+    UP, LOW = pl.ds(0, 64), pl.ds(64, 64)
+
+    class Gather:
+        def __init__(self, buf):
+            self.buf = buf
+            self.a, self.b = sems(10)
+
+        def copy(self, n):
+            ly, lw = 4 * (1 - y) + 2 * w + c, 4 * y + 2 * (1 - w) + c
+            ld = 4 * (1 - y) + 2 * (1 - w) + c
+            from_row, rows, device = (
+                (ROWS * lane, 128, sibling),
+                (ROWS * lane, 64, y_nbr), (ROWS * lane + 64, 64, y_nbr),
+                (ROWS * lane + 64, 64, w_nbr), (ROWS * lane, 64, w_nbr),
+                (ROWS * ly, 64, w_nbr), (ROWS * lw + 64, 64, y_nbr),
+                (ROWS * ly, 128, sibling), (ROWS * lw, 128, sibling), (ROWS * ld, 128, sibling),
+            )[n]
+            ref = self.buf.at[pl.ds(pl.multiple_of(from_row, 64), rows)]
+            return rc(ref, ref, self.a + n, self.b + n, device)
+
+        def start(self):
+            begun(self)
+            self.passed = False
+            for n in (1, 3, 2, 4, 0):
+                self.copy(n).start()
+
+        def pass_on(self):
+            self.passed = True
+            for n, then in ((1, 5), (3, 6), (2, 7), (4, 8), (5, None), (6, 9)):
+                self.copy(n).wait_recv()
+                if then is not None:
+                    self.copy(then).start()
+
+        def wait(self):
+            if not self.passed:
+                self.pass_on()
+            self.got = True
+            for n in (0, 7, 8, 9):
+                self.copy(n).wait_recv()
+
+        def drain(self):
+            for n in range(10):
+                self.copy(n).wait_send()
+
+    class Scatter:
+        def __init__(self, slot, partial):
+            self.slot = slot
+            self.partial = partial
+            self.a1, self.b1 = sems(4)
+            self.a2, self.b2 = sems(6)
+
+        def far(self, i):
+            dy, dw = i // 2, i % 2
+            y_, w_ = y + dy - 2 * y * dy, w + dw - 2 * w * dw
+            return y_, w_
+
+        def first(self, i):
+            return rc(rs_s1.at[self.slot, i], rs_r1.at[self.slot, i], self.a1 + i, self.b1 + i, sibling)
+
+        def second(self, n):
+            src, half, dst, half_there, device = (
+                (2, UP, 2, UP, y_nbr), (2, LOW, 2, LOW, w_nbr),
+                (0, UP, 0, UP, y_nbr), (1, LOW, 1, LOW, w_nbr),
+                (0, LOW, 0, LOW, y_nbr), (1, UP, 1, UP, w_nbr),
+            )[n]
+            return rc(rs_s2.at[self.slot, src, half], rs_r2.at[self.slot, dst, half_there], self.a2 + n, self.b2 + n, device)
+
+        def start(self, hold=False):
+            begun(self)
+            self.passed = False
+
+            @pl.loop(0, 4)
+            def _(n):
+                i = 3 - n
+                y_, w_ = self.far(i)
+                rs_s1[self.slot, i] = self.partial(4 * y_ + 2 * w_ + 1 - c).astype(BF)
+                self.first(i).start()
+
+            def total(i):
+                y_, w_ = self.far(i)
+                part = self.partial(4 * y_ + 2 * w_ + c)
+                self.first(i).wait_recv()
+                return part + rs_r1[self.slot, i].astype(F32)
+
+            rs_s2[self.slot, 2] = total(3).astype(BF)
+            if not hold:
+                self.second(0).start()
+                self.second(1).start()
+            value = total(2)
+            rs_s2[self.slot, 0, 0:64] = value[0:64].astype(BF)
+            if not hold:
+                self.second(2).start()
+            kept[self.slot, 0] = value[64:128]
+            value = total(1)
+            rs_s2[self.slot, 1, 64:128] = value[64:128].astype(BF)
+            if not hold:
+                self.second(3).start()
+            kept[self.slot, 1] = value[0:64]
+            own[self.slot] = total(0)
+
+        def release(self):
+            for n in range(4):
+                self.second(n).start()
+
+        def pass_on(self):
+            self.passed = True
+            self.second(0).wait_recv()
+            rs_s2[self.slot, 1, 0:64] = (kept[self.slot, 1] + rs_r2[self.slot, 2, 0:64].astype(F32)).astype(BF)
+            self.second(5).start()
+            self.second(1).wait_recv()
+            rs_s2[self.slot, 0, 64:128] = (kept[self.slot, 0] + rs_r2[self.slot, 2, 64:128].astype(F32)).astype(BF)
+            self.second(4).start()
+
+        def wait(self):
+            if not self.passed:
+                self.pass_on()
+            self.got = True
+            for n in (2, 3, 4, 5):
+                self.second(n).wait_recv()
+            return own[self.slot] + rs_r2[self.slot, 0].astype(F32) + rs_r2[self.slot, 1].astype(F32)
+
+        def drain(self):
+            for i in range(4):
+                self.first(i).wait_send()
+            for n in range(6):
+                self.second(n).wait_send()
+
+    class Batch:
+        def __init__(self, copies):
+            self.copies = copies
+            self.a, self.b = sems(len(copies))
+
+        def copy(self, n):
+            src, dst, device = self.copies[n]
+            return rc(src, dst, self.a + n, self.b + n, device)
+
+        def start(self):
+            begun(self)
+            for n in range(len(self.copies)):
+                self.copy(n).start()
+
+        def wait(self):
+            self.got = True
+            for n in range(len(self.copies)):
+                self.copy(n).wait_recv()
+
+        def drain(self):
+            for n in range(len(self.copies)):
+                self.copy(n).wait_send()
+
+    hx, hk = x + w - 2 * x * w, k + c - 2 * k * c
+    z_dev, x_dev = partner((0, 1))[3], partner((1, 0))[3]
+
+    class Across:
+        def __init__(self, views):
+            self.views = views
+            self.n = len(views(x, k))
+            self.a, self.b = sems(3 * self.n)
+
+        def copies(self, leg):
+            refs = self.views(x, 1 - k) if leg == 2 else self.views(x, k)
+            at = self.n * leg
+            return [rc(v, v, self.a + at + i, self.b + at + i, z_dev if leg == 0 else x_dev) for i, v in enumerate(refs)]
+
+        def arrivals(self, leg):
+            refs = self.views(*((x, 1 - k), (1 - x, k), (1 - x, 1 - k))[leg])
+            at = self.n * leg
+            return [rc(v, v, self.a + at + i, self.b + at + i, z_dev if leg == 0 else x_dev) for i, v in enumerate(refs)]
+
+        def start(self):
+            begun(self)
+            self.passed = False
+            for leg in (0, 1):
+                for copy in self.copies(leg):
+                    copy.start()
+
+        def pass_on(self):
+            self.passed = True
+            for copy in self.arrivals(0):
+                copy.wait_recv()
+            for copy in self.copies(2):
+                copy.start()
+
+        def wait(self):
+            if not self.passed:
+                self.pass_on()
+            self.got = True
+            for leg in (1, 2):
+                for copy in self.arrivals(leg):
+                    copy.wait_recv()
+
+        def drain(self):
+            for leg in range(3):
+                for copy in self.copies(leg):
+                    copy.wait_send()
+
+    class Reduce:
+        def __init__(self, grad, rx, sz, rz):
+            self.grad, self.rx, self.sz, self.rz = grad, rx, sz, rz
+            self.runs = rx.shape[0]
+            self.a, self.b = sems(self.runs + 1)
+
+        def run(self, n):
+            return rc(self.grad.at[many(512 * n + 256 * (1 - x), 256)], self.rx.at[n], self.a + n, self.b + n, x_dev)
+
+        def last(self):
+            return rc(self.sz, self.rz, self.a + self.runs, self.b + self.runs, z_dev)
+
+        def start(self):
+            begun(self)
+            self.passed = False
+            for n in range(self.runs):
+                self.run(n).start()
+
+        def part(self, n, k_):
+            return (
+                self.grad[many(512 * n + 256 * x + 128 * k_, 128), :].astype(F32)
+                + self.rx[n, many(128 * k_, 128), :].astype(F32)
+            )
+
+        def pass_on(self):
+            self.passed = True
+            for n in range(self.runs):
+                self.run(n).wait_recv()
+            for n in range(self.runs):
+                self.sz[n] = self.part(n, 1 - k).astype(BF)
+            self.last().start()
+
+        def wait(self):
+            if not self.passed:
+                self.pass_on()
+            self.got = True
+            self.last().wait_recv()
+
+        def total(self, n):
+            return self.part(n, k) + self.rz[n].astype(F32)
+
+        def drain(self):
+            for n in range(self.runs):
+                self.run(n).wait_send()
+            self.last().wait_send()
+
+    swap_rows = many(ROWS * (4 * k + 2 * w + c), ROWS)
+    tok_swap = Swap(tokens, tok_all.at[swap_rows])
+    cot_swap = Swap(cot, cot_all.at[swap_rows])
+    tok_swap.start()
     own_rows = many(32 * idx, 32)
+
+    def up_cols(r, y_, w_, c_):
+        return many(128 * (16 * y_ + 8 * (r // 2) + 4 * (r % 2) + 2 * w_ + c_), 128)
+
     copies = []
     for d in group:
         y_, w_, c_, l_, dv = peer(d)
@@ -742,25 +780,7 @@
         for p in range(3):
             copies.append((wqkv_in.at[:, many(128 * (8 * p + l_), 128)], wqkv.at[own_rows, pl.ds(128 * p, 128)], dv))
     in_qkv = Batch(copies)
-    copies = []
-    for d in group:
-        y_, w_, c_, l_, dv = peer(d)
-        for r in range(4):
-            copies.append((wup_in.at[:, many(128 * (16 * y_ + 8 * (r // 2) + 4 * (r % 2) + 2 * w_ + c_), 128)], wup.at[own_rows, pl.ds(128 * r, 128)], dv))
-    in_up = Batch(copies)
     in_qkv.start()
-
-    @pl.when(off_diag == 0)
-    def _():
-        tok_all[my_rows, :] = tokens[...]
-
-    pack_all[idx] = pack_in[...]
-    for p in range(3):
-        wqkv[own_rows, 128 * p : 128 * p + 128] = wqkv_in[:, many(128 * (8 * p + lane), 128)]
-
-    tok_swap.wait()
-    tok = Gather(tok_all)
-    tok.start()
 
     out_a, out_b = sems(4)
     place = 2 * w + c
@@ -773,13 +793,35 @@
         m = 2 * flip(w, dw) + flip(c, dc)
         out_in.append(rc(wout_in, wout.at[many(32 * m, 32)], out_a, out_b + m, home_dev))
     to_home = Only(away, [rc(wout_in, wout.at[out_rows], out_a, out_b + place, home_dev)], is_home, out_in)
+    copies = []
+    for d in group:
+        y_, w_, c_, l_, dv = peer(d)
+        for r in range(4):
+            copies.append((wup_in.at[:, up_cols(r, y_, w_, c_)], wup.at[own_rows, pl.ds(128 * r, 128)], dv))
+    in_up = Batch(copies)
+    in_up.start()
     to_home.start()
+
+    @pl.when(off_diag == 0)
+    def _():
+        tok_all[my_rows, :] = tokens[...]
+
+    pack_all[idx] = pack_in[...]
+    for p in range(3):
+        wqkv[own_rows, 128 * p : 128 * p + 128] = wqkv_in[:, many(128 * (8 * p + lane), 128)]
+    for r in range(4):
+        wup[own_rows, 128 * r : 128 * r + 128] = wup_in[:, up_cols(r, y, w, c)]
 
     @pl.when(is_home == 1)
     def _():
         wout[out_rows, :] = wout_in[...]
 
-    in_qkv.wait()
+    for load in loads[4:]:
+        load.wait()
+
+    @pl.when(off_diag == 0)
+    def _():
+        cot_all[my_rows, :] = cot[...]
 
     def runs_of(ref, *more):
         def views(x_, k_):
@@ -788,20 +830,15 @@
 
         return views
 
-    rank_rows = many(128 * rank, 128)
     dp_qkv = Across(runs_of(wqkv, pack_all))
     dp_up = Across(runs_of(wup))
     dp_down = Across(lambda x_, k_: [wdown.at[many(128 * (2 * x_ + k_), 128)]])
+    in_qkv.wait()
     dp_qkv.start()
+    tok_swap.wait()
+    tok = Gather(tok_all)
+    tok.start()
     cot_swap.start()
-    in_up.start()
-    for r in range(4):
-        wup[own_rows, 128 * r : 128 * r + 128] = wup_in[:, many(128 * (16 * y + 8 * (r // 2) + 4 * (r % 2) + 2 * w + c), 128)]
-    wdown[rank_rows, :] = wdown_in[...]
-
-    @pl.when(off_diag == 0)
-    def _():
-        cot_all[my_rows, :] = cot[...]
 
     dpo_a, dpo_b = sems(2)
     out_z_copy = rc(wout, wout, dpo_a, dpo_b, z_dev)
@@ -809,17 +846,11 @@
     dp_out = Only(is_home, [out_z_copy, out_x_copy], (1 - hx) * hk, [out_z_copy])
     dp_out_more = Only((1 - hx) * hk, [out_x_copy], hx, [out_x_copy])
     to_home.wait()
+    in_up.wait()
+    dp_qkv.pass_on()
     dp_out.start()
+    dp_up.start()
     tok.pass_on()
-    in_up.wait()
-    dp_up.start()
-    dp_qkv.pass_on()
-    dp_out.wait()
-    dp_out_more.start()
-    dp_down.start()
-    cot_swap.wait()
-    cg = Gather(cot_all)
-    cg.start()
 
     dp_qkv.wait()
     lane_id = lax.broadcasted_iota(jnp.int32, (16, 128), 1)
@@ -866,6 +897,12 @@
         v_s[rows, :] = (proj[:, 256:384] + bias_v).astype(BF)
 
     QB = 256
+    cot_swap.wait()
+    cg = Gather(cot_all)
+    cg.start()
+    dp_down.start()
+    dp_out.wait()
+    dp_out_more.start()
     head_lane = lax.broadcasted_iota(jnp.int32, (1, 128), 1) // 64
 
     def of_head(v, h):
@@ -892,12 +929,12 @@
     def rows_of(l_):
         return many(ROWS * l_, ROWS)
 
-    cg.pass_on()
     rs_out = Scatter(0, lambda l_: dot_nn(att[rows_of(l_), :], wout[...]))
     rs_out.start()
-
+    rs_out.pass_on()
+
+    cg.pass_on()
     dp_up.pass_on()
-    dp_down.pass_on()
 
     stream = tok_all[my_rows, :].astype(F32) + extra
     mid = stream + (rs_out.wait() + bias_out)
@@ -906,6 +943,7 @@
     n2_all[my_rows, :] = (xhat2 * gain1 + shift1).astype(BF)
     n2 = Gather(n2_all)
     n2.start()
+    dp_down.pass_on()
     n2.pass_on()
     dp_up.wait()
     dp_down.wait()
@@ -935,6 +973,7 @@
 
     down_red = Reduce(gdown, xdown, zdown_s, zdown)
     down_red.start()
+    rs_n2.pass_on()
     upb_sends = Batch([(upb_g.at[:, many(128 * partner(d)[2], 128)], r_upb.at[n], partner(d)[3]) for n, d in enumerate(ranks)])
     upb_sends.start()
 
@@ -946,6 +985,8 @@
     up_red = Reduce(gup, xup, zup_s, zup)
     up_red.start()
 
+    rs_mix = Scatter(2, lambda l_: dot_nn(act[rows_of(l_), :], wdown[...]))
+    rs_mix.start(hold=True)
     n2_grad = rs_n2.wait()
     incoming = cot_all[my_rows, :].astype(F32)
     xhat2, rstd2 = center(middle[...])
@@ -954,6 +995,7 @@
     ml_all[my_rows, :] = mg.astype(BF)
     ml = Gather(ml_all)
     ml.start()
+    smallp[7:16, :] = jnp.zeros((9, D), F32)
     smallp[2:3, :] = jnp.sum(n2_grad * xhat2, axis=0, keepdims=True)
     smallp[4:5, :] = jnp.sum(n2_grad, axis=0, keepdims=True)
     smallp[5:6, :] = jnp.sum(mg.astype(BF).astype(F32), axis=0, keepdims=True)
@@ -963,8 +1005,7 @@
     ml.pass_on()
     up_red.pass_on()
     ml.wait()
-    rs_mix = Scatter(2, lambda l_: dot_nn(act[rows_of(l_), :], wdown[...]))
-    rs_mix.start()
+    rs_mix.release()
 
     @pl.loop(0, 4)
     def _(n):
@@ -974,8 +1015,7 @@
     dk_acc[...] = jnp.zeros_like(dk_acc)
     dv_acc[...] = jnp.zeros_like(dv_acc)
 
-    @pl.loop(0, D // QB)
-    def _(n):
+    def attend_back(n):
         rows = many(QB * n, QB)
         queries = q_s[rows, :]
         grads = dog[rows, :]
@@ -992,9 +1032,15 @@
             dv_acc[...] += dot_tn(share, of_head(grads, h))
         dproj[rows, 0:128] = (dq.astype(BF).astype(F32) * 0.125).astype(BF)
 
+    pl.loop(0, 2)(attend_back)
+    rs_mix.pass_on()
+    pl.loop(2, 4)(attend_back)
     dproj[:, 128:256] = dk_acc[...].astype(BF)
     dproj[:, 256:384] = dv_acc[...].astype(BF)
 
+    low = dproj[...].astype(F32)
+    smallp[8:9, lane_cols] = jnp.sum(low[:, 0:128], axis=0, keepdims=True)
+    smallp[9:10, lane_cols] = jnp.sum(low[:, 256:384], axis=0, keepdims=True)
     rs_n1 = Scatter(3, lambda l_: dot_nt(dproj[rows_of(l_), :], wqkv[...]))
     rs_n1.start()
 
@@ -1005,6 +1051,7 @@
 
     qkv_red = Reduce(gqkv, xqkv, zqkv_s, zqkv)
     qkv_red.start()
+    rs_n1.pass_on()
     gout[...] = dot_tn(att[...], ml_all[...]).astype(BF)
     go_a, go_b = sems(2)
     grad_x = Only(hx, [rc(gout, out_x, go_a, go_b, x_dev)], 1 - hx, [rc(gout, out_x, go_a, go_b, x_dev)])
@@ -1027,27 +1074,31 @@
     xhat1, rstd1 = center(tok_all[my_rows, :].astype(F32) + extra)
     tg = mgrad[...] + norm_back(xhat1, rstd1, gain0, n1_grad)
     tgr[0] = tg.astype(BF)
-    tg_swap = Swap(tgr.at[0], tgr.at[1])
-    tg_swap.start()
     smallp[0:1, :] = jnp.sum(tg, axis=0, keepdims=True)
     smallp[1:2, :] = jnp.sum(n1_grad * xhat1, axis=0, keepdims=True)
     smallp[3:4, :] = jnp.sum(n1_grad, axis=0, keepdims=True)
-    smallp[7:8, :] = jnp.zeros((1, D), F32)
-
-    small_group = Batch([(smallp.at[:, many(128 * peer(d)[3], 128)], r_a.at[n], peer(d)[4]) for n, d in enumerate(group)])
+
+    def block(y_, x_, k_):
+        return smallp.at[:, many(128 * (4 * y_ + 2 * x_ + k_), 128)]
+
+    copies = []
+    for n, d in enumerate(ranks):
+        x_, k_, r_, dv = partner(d)
+        for y_ in range(2):
+            copies.append((block(y_, x_, k_), r_b.at[n, y_], dv))
+    small_ranks = Batch(copies)
+    small_ranks.start()
+    tg_swap = Swap(tgr.at[0], tgr.at[1])
+    tg_swap.start()
+    small_ranks.wait()
+    for y_ in range(2):
+        first = smallp[:, many(128 * (4 * y_ + 2 * x + k), 128)]
+        s_b[y_, 0:1, :] = first[0:1, :]
+        for n in range(3):
+            s_b[y_, n + 1 : n + 2, :] = r_b[n, y_, 0:1, :]
+        s_b[y_, 4:16, :] = (first + r_b[0, y_] + r_b[1, y_] + r_b[2, y_])[1:13, :]
+    small_group = Batch([(s_b.at[peer(d)[0]], r_a.at[n], peer(d)[4]) for n, d in enumerate(group)])
     small_group.start()
-
-    small_group.wait()
-    total = smallp[:, lane_cols]
-    for n in range(7):
-        total = total + r_a[n]
-    s_b[0:8, :] = total
-    low = dproj[...].astype(F32)
-    s_b[8:9, :] = jnp.sum(low[:, 0:128], axis=0, keepdims=True)
-    s_b[9:10, :] = jnp.sum(low[:, 256:384], axis=0, keepdims=True)
-    s_b[10:16, :] = jnp.zeros((6, 128), F32)
-    small_ranks = Batch([(s_b, r_b.at[n], partner(d)[3]) for n, d in enumerate(ranks)])
-    small_ranks.start()
 
     down_red.wait()
     gd_o[...] = down_red.total(0).astype(BF)
@@ -1085,40 +1136,20 @@
     out_deal.start()
     qkv_deal = collect(qkv_red, sq2, rq2)
 
-    small_ranks.wait()
-    blocks = [None] * 4
-    rows_sum = s_b[...]
-    for n in range(3):
-        rows_sum = rows_sum + r_b[n]
+    small_group.wait()
+    total = s_b[y]
+    for n in range(7):
+        total = total + r_a[n]
     own_facts = [facts] + [pack_all[8 * (2 * partner(d)[1] + partner(d)[0])].astype(F32)[17:18, :] for d in ranks]
-    own_sums = [s_b[0:1, :]] + [r_b[n, 0:1, :] for n in range(3)]
-    facts8 = jnp.concatenate(own_facts + [jnp.zeros((4, 128), F32)], axis=0)
-    facts_t = jnp.transpose(facts8)
+    facts_t = jnp.transpose(jnp.concatenate(own_facts + [jnp.zeros((4, 128), F32)], axis=0))
     table = None
     for n in range(4):
-        part = facts_t[:, n : n + 1] * own_sums[n]
+        part = facts_t[:, n : n + 1] * total[n : n + 1, :]
         table = part if table is None else table + part
-    s_a[0:64, :] = table[0:64, :]
-    s_a[64:80, :] = rows_sum
-    s_a[80:81, :] = table[64:65, :] * hours_scale
-    s_a[81:88, :] = jnp.zeros((7, 128), F32)
-    sm_a, sm_b = sems(3)
-    copies = []
-    for n, (dw, dc) in enumerate(pairs):
-        w_, c_ = flip(w, dw), flip(c, dc)
-        copies.append(rc(s_a, r_c, sm_a + n, sm_b, dev(y, x, k, w_, c_)))
-    small_deal = Only(is_home, copies, away, [rc(s_a, r_c, sm_a, sm_b, home_dev)])
-    small_deal.start()
-    small_deal.wait()
-
-    @pl.when(is_home == 1)
-    def _():
-        small_o[0:88, :] = s_a[...]
-
-    @pl.when(is_home == 0)
-    def _():
-        small_o[0:88, :] = r_c[...]
-
+    small_o[0:64, :] = table[0:64, :]
+    small_o[64:80, :] = total
+    small_o[80:81, :] = table[64:65, :] * hours_scale
+    small_o[81:88, :] = jnp.zeros((7, 128), F32)
     upb_sends.wait()
     sum_upb = upb_g[:, rank_rows]
     for n in range(3):
@@ -1176,10 +1207,10 @@
     for m in range(1, 4):
         mine = jnp.where(place == m, pltpu.roll(small, 128 - 32 * m, 1), mine)
     table_o[...] = mine[0:48, 0:32]
-    gain_o[...] = mine[65:67, 0:32]
-    shift_o[...] = mine[67:69, 0:32]
-    bias_o[...] = mine[69:71, 0:32]
-    qv_o[...] = mine[72:74, 0:32]
+    gain_o[...] = mine[68:70, 0:32]
+    shift_o[...] = mine[70:72, 0:32]
+    bias_o[...] = mine[72:74, 0:32]
+    qv_o[...] = mine[75:77, 0:32]
     lead_o[...] = mine[80:81, 0:32]
     upb_o[...] = small_i[88:89, :]
 
@@ -1190,10 +1221,11 @@
 ):
     vm = pltpu.VMEM
     scratch = [
+        vm((128, D), BF), vm((32, 3 * D), BF), vm((32, 4 * D), BF), vm((32, D), BF), vm((128, D), BF),
         vm((D, D), BF), vm((D, D), BF), vm((D, D), BF), vm((D, D), BF),
         vm((D, 384), BF), vm((D, FFL), BF), vm((FFL, D), BF), vm((128, D), BF), vm((80, 128), F32), vm((32, 128), BF), vm((32, 32, 128), BF), vm((64, D), F32),
         vm((D, D), BF), vm((D, 128), BF), vm((D, 128), BF), vm((D, 128), BF), vm((2, D, D), BF), vm((D, 128), F32), vm((D, 128), BF),
-        vm((4, 4, 128, D), BF), vm((4, 4, 128, D), BF), vm((4, 3, 128, D), BF), vm((4, 3, 128, D), BF), vm((4, 128, D), F32),
+        vm((4, 4, 128, D), BF), vm((4, 4, 128, D), BF), vm((4, 3, 128, D), BF), vm((4, 3, 128, D), BF), vm((4, 128, D), F32), vm((4, 2, 64, D), F32),
         vm((128, D), F32), vm((128, D), F32), vm((D, FFL), BF), vm((D, FFL), BF), vm((D, 384), BF), vm((D, 128), BF), vm((D, 128), F32), vm((D, 128), F32),
         vm((D, 384), BF), vm((D, FFL), BF), vm((FFL, D), BF), vm((128, D), BF),
         vm((2, 256, 384), BF), vm((2, 256, FFL), BF), vm((1, 256, D), BF),
@@ -1201,9 +1233,9 @@
         vm((2, 128, 384), BF), vm((2, 128, FFL), BF), vm((1, 128, D), BF),
         vm((128, D), BF), vm((128, D), BF), vm((128, D), BF),
         vm((256, 384), BF), vm((256, FFL), BF), vm((8, 32, 384), BF), vm((8, 32, FFL), BF), vm((128, D), BF), vm((32, D), BF),
-        vm((4, 128, D), BF), vm((8, D), F32), vm((88, 128), F32), vm((7, 8, 128), F32), vm((16, 128), F32), vm((3, 16, 128), F32), vm((88, 128), F32),
+        vm((4, 128, D), BF), vm((16, D), F32), vm((7, 16, 128), F32), vm((2, 16, 128), F32), vm((3, 2, 16, 128), F32),
         vm((8, FFL), F32), vm((3, 8, 128), F32),
-        pltpu.SemaphoreType.DMA((260,)), pltpu.SemaphoreType.DMA((260,)),
+        pltpu.SemaphoreType.DMA((320,)), pltpu.SemaphoreType.DMA((320,)), pltpu.SemaphoreType.DMA((8,)),
     ]
     shape = jax.ShapeDtypeStruct
     raw = pl.pallas_call(
@@ -1212,7 +1244,7 @@
             shape((128, D), BF), shape((128, D), BF), shape((8, 32, 384), BF), shape((32, D), BF), shape((8, 32, FFL), BF),
             shape((128, D), BF), shape((96, 128), F32),
         ],
-        in_specs=[pl.BlockSpec(memory_space=vm)] * 15,
+        in_specs=[pl.BlockSpec(memory_space=pl.ANY if n in (0, 7, 9, 11, 13, 14) else vm) for n in range(15)],
         out_specs=[pl.BlockSpec(memory_space=vm)] * 7,
         scratch_shapes=scratch,
         compiler_params=pltpu.CompilerParams(collective_id=0, has_side_effects=True, vmem_limit_bytes=62 * 2**20),
@@ -1230,7 +1262,7 @@
         ],
         in_specs=[pl.BlockSpec(memory_space=vm)] * 7,
         out_specs=[pl.BlockSpec(memory_space=vm)] * 13,
-        compiler_params=pltpu.CompilerParams(vmem_limit_bytes=32 * 2**20),
+        compiler_params=pltpu.CompilerParams(vmem_limit_bytes=62 * 2**20),
         cost_estimate=pl.CostEstimate(flops=1_000_000, bytes_accessed=4_000_000, transcendentals=0),
     )(*raw)
     mixed, tg, table, lead, gain, shift, gq, qv, go, bias, gu, upb, gd = out

time: 222 us -> 206 us (0.928)
  Pallas kernels: 212 us -> 202 us
  local copies, waits for them, and re-layouts: 7.75 us -> 2.13 us
    pallas_call x1, Pallas kernels: 211 us -> 199 us  [local_fast(): pl.pallas_call(fast_kernel, out_shape=[shape((128, D), BF), shape((128, D...]
    unnamed x18 -> x6, local copies, waits for them, and re-layouts: 7.75 us -> 2.13 us
where the time goes in v3:
time: 206 us; the launch traced here: 205 us
  Pallas kernels  202 us (98%)
  local copies, waits for them, and re-layouts  2.13 us (1%)
    pallas_call x1, Pallas kernels, local_fast(): pl.pallas_call(fast_kernel, out_shape=[shape((128, D), BF), shape((128, D...  199 us

profile of v3, /device:TPU:0, one launch (start us, length us, event | category | flops | bytes accessed | tf_op | source)
XLA Modules:
  0.0 205.4 jit_solution(2903226131859068383)
XLA Ops:
  0.6 0.0 copy-start.1
  1.3 0.0 copy-done.1
  1.3 0.7 copy.28.var_table
  2.0 199.2 %shard_map.246 = (bf16[128,1024]{1,0:T(8,128)(2,1)}, bf16[128,1024]{1,0:T(8,128)(2,1)}, bf16[8,32,384]{2,1,0:T(8,128)(2,1)}, bf16[32,1024]{1,0:T(8,128)(2,1)}, b...) custom-call(bf16[128,1024]{1,0:T(8,128)(2,1)} %bitcast.8, s32[1,1]{1,0:T(1,128)} %bitcast.7.lead_hours, ...), custom_call_target="tpu_custom_call" | custom-call | flops 14000000000 | bytes 4000000 | tf_op jit(solution)/shard_map/pallas_call | solution.py:1241
  201.2 2.8 %shard_map.247 = (bf16[1,128,1024]{2,1,0:T(8,128)(2,1)}, f32[1,128,1024]{2,1,0:T(8,128)}, f32[48,32]{1,0:T(8,128)}, f32[1,32]{1,0:T(1,128)}, f32[2,32]{1,0:T(2,1...) custom-call(bf16[128,1024]{1,0:T(8,128)(2,1)} %get-tuple-element.33., ...), custom_call_target="tpu_custom_call" | custom-call | flops 1000000 | bytes 4000000 | tf_op jit(solution)/shard_map/pallas_call | solution.py:1256
  204.0 0.0 copy-start
  204.0 0.7 copy-done
  204.7 0.7 copy.29
Async XLA Ops:
  0.6 0.7 copy-start.1
  204.0 0.7 copy-start

commit v4 on v3

--- a/solution.py
+++ b/solution.py
@@ -383,9 +383,10 @@
 
 
 def fast_kernel(
-    tokens_h, lead_hours, var_mask, var_table, lead_weight, norm_gain, norm_shift, wqkv_h, qv_bias, wout_h,
-    branch_bias, wup_h, up_bias, wdown_h, cot_h,
+    tokens_h, lead_hours_h, var_mask_h, var_table_h, lead_weight_h, norm_gain_h, norm_shift_h, wqkv_h, qv_bias_h, wout_h,
+    branch_bias_h, wup_h, up_bias_h, wdown_h, cot_h,
     mixed_o, tg_o, gq_o, go_o, gu_o, gd_o, small_o,
+    lead_hours, var_mask, var_table, lead_weight, norm_gain, norm_shift, qv_bias, branch_bias, up_bias,
     tokens, wqkv_in, wup_in, wout_in, cot, tok_all, cot_all, n2_all, ml_all,
     wqkv, wup, wdown, wout, raw, pack_in, pack_all, full,
     normed, q_s, k_s, v_s, shares, attf, att,
@@ -455,9 +456,18 @@
         pltpu.make_async_copy(src, dst, ls.at[n])
         for n, (src, dst) in enumerate(((tokens_h, tokens), (wqkv_h, wqkv_in), (wup_h, wup_in), (wout_h, wout_in), (cot_h, cot), (wdown_h, wdown.at[rank_rows])))
     ]
-    for load in loads:
+    small_loads = [
+        pltpu.make_async_copy(src, dst, ls.at[8 + n])
+        for n, (src, dst) in enumerate((
+            (lead_hours_h, lead_hours), (var_mask_h, var_mask), (var_table_h, var_table), (lead_weight_h, lead_weight),
+            (norm_gain_h, norm_gain), (norm_shift_h, norm_shift), (qv_bias_h, qv_bias), (branch_bias_h, branch_bias), (up_bias_h, up_bias),
+        ))
+    ]
+    for load in small_loads + loads:
         load.start()
     raw[...] = jnp.zeros_like(raw)
+    for load in small_loads:
+        load.wait()
     raw[0:48, 0:32] = var_table[...].astype(F32)
     for n, rows in ((48, norm_gain), (50, norm_shift), (52, qv_bias), (54, branch_bias)):
         raw[n : n + 2, 0:32] = rows[...].astype(F32)
@@ -952,9 +962,9 @@
 
     upb_g[...] = jnp.zeros_like(upb_g)
 
-    @pl.loop(0, 8)
+    @pl.loop(0, 4)
     def _(n):
-        rows = many(128 * n, 128)
+        rows = many(256 * n, 256)
         up = dot_nn(n2_all[rows, :], wup[...]) + bias_up
         cdf = 0.5 * (1.0 + erf(up * 0.7071067811865476))
         act[rows, :] = (up * cdf).astype(BF)
@@ -986,7 +996,7 @@
     up_red.start()
 
     rs_mix = Scatter(2, lambda l_: dot_nn(act[rows_of(l_), :], wdown[...]))
-    rs_mix.start(hold=True)
+    rs_mix.start()
     n2_grad = rs_n2.wait()
     incoming = cot_all[my_rows, :].astype(F32)
     xhat2, rstd2 = center(middle[...])
@@ -995,6 +1005,7 @@
     ml_all[my_rows, :] = mg.astype(BF)
     ml = Gather(ml_all)
     ml.start()
+    rs_mix.pass_on()
     smallp[7:16, :] = jnp.zeros((9, D), F32)
     smallp[2:3, :] = jnp.sum(n2_grad * xhat2, axis=0, keepdims=True)
     smallp[4:5, :] = jnp.sum(n2_grad, axis=0, keepdims=True)
@@ -1005,7 +1016,10 @@
     ml.pass_on()
     up_red.pass_on()
     ml.wait()
-    rs_mix.release()
+    mixed_low = (middle[...] + (rs_mix.wait() + bias_down)).astype(BF)
+    tgr[2] = mixed_low
+    mix_swap = Swap(tgr.at[2], tgr.at[3])
+    mix_swap.start()
 
     @pl.loop(0, 4)
     def _(n):
@@ -1033,34 +1047,29 @@
         dproj[rows, 0:128] = (dq.astype(BF).astype(F32) * 0.125).astype(BF)
 
     pl.loop(0, 2)(attend_back)
-    rs_mix.pass_on()
     pl.loop(2, 4)(attend_back)
     dproj[:, 128:256] = dk_acc[...].astype(BF)
     dproj[:, 256:384] = dv_acc[...].astype(BF)
 
+    @pl.loop(0, 4)
+    def _(n):
+        cols = many(256 * n, 256)
+        gqkv[cols, :] = dot_tn(normed[:, cols], dproj[...]).astype(BF)
+
+    qkv_red = Reduce(gqkv, xqkv, zqkv_s, zqkv)
+    qkv_red.start()
     low = dproj[...].astype(F32)
     smallp[8:9, lane_cols] = jnp.sum(low[:, 0:128], axis=0, keepdims=True)
     smallp[9:10, lane_cols] = jnp.sum(low[:, 256:384], axis=0, keepdims=True)
     rs_n1 = Scatter(3, lambda l_: dot_nt(dproj[rows_of(l_), :], wqkv[...]))
     rs_n1.start()
 
-    @pl.loop(0, 4)
-    def _(n):
-        cols = many(256 * n, 256)
-        gqkv[cols, :] = dot_tn(normed[:, cols], dproj[...]).astype(BF)
-
-    qkv_red = Reduce(gqkv, xqkv, zqkv_s, zqkv)
-    qkv_red.start()
     rs_n1.pass_on()
     gout[...] = dot_tn(att[...], ml_all[...]).astype(BF)
     go_a, go_b = sems(2)
     grad_x = Only(hx, [rc(gout, out_x, go_a, go_b, x_dev)], 1 - hx, [rc(gout, out_x, go_a, go_b, x_dev)])
     grad_z = Only((1 - hx) * hk, [rc(out_s, out_z, go_a + 1, go_b + 1, z_dev)], is_home, [rc(out_s, out_z, go_a + 1, go_b + 1, z_dev)])
     grad_x.start()
-    mixed_low = (middle[...] + (rs_mix.wait() + bias_down)).astype(BF)
-    tgr[2] = mixed_low
-    mix_swap = Swap(tgr.at[2], tgr.at[3])
-    mix_swap.start()
     qkv_red.pass_on()
     grad_x.wait()
 
@@ -1221,6 +1230,8 @@
 ):
     vm = pltpu.VMEM
     scratch = [
+        vm((1, 1), jnp.int32), vm((1, 48), jnp.int32), vm((48, 32), BF), vm((1, 32), BF), vm((2, 32), BF), vm((2, 32), BF),
+        vm((2, 32), BF), vm((2, 32), BF), vm((1, 128), BF),
         vm((128, D), BF), vm((32, 3 * D), BF), vm((32, 4 * D), BF), vm((32, D), BF), vm((128, D), BF),
         vm((D, D), BF), vm((D, D), BF), vm((D, D), BF), vm((D, D), BF),
         vm((D, 384), BF), vm((D, FFL), BF), vm((FFL, D), BF), vm((128, D), BF), vm((80, 128), F32), vm((32, 128), BF), vm((32, 32, 128), BF), vm((64, D), F32),
@@ -1235,7 +1246,7 @@
         vm((256, 384), BF), vm((256, FFL), BF), vm((8, 32, 384), BF), vm((8, 32, FFL), BF), vm((128, D), BF), vm((32, D), BF),
         vm((4, 128, D), BF), vm((16, D), F32), vm((7, 16, 128), F32), vm((2, 16, 128), F32), vm((3, 2, 16, 128), F32),
         vm((8, FFL), F32), vm((3, 8, 128), F32),
-        pltpu.SemaphoreType.DMA((320,)), pltpu.SemaphoreType.DMA((320,)), pltpu.SemaphoreType.DMA((8,)),
+        pltpu.SemaphoreType.DMA((320,)), pltpu.SemaphoreType.DMA((320,)), pltpu.SemaphoreType.DMA((24,)),
     ]
     shape = jax.ShapeDtypeStruct
     raw = pl.pallas_call(
@@ -1244,7 +1255,7 @@
             shape((128, D), BF), shape((128, D), BF), shape((8, 32, 384), BF), shape((32, D), BF), shape((8, 32, FFL), BF),
             shape((128, D), BF), shape((96, 128), F32),
         ],
-        in_specs=[pl.BlockSpec(memory_space=pl.ANY if n in (0, 7, 9, 11, 13, 14) else vm) for n in range(15)],
+        in_specs=[pl.BlockSpec(memory_space=pl.ANY)] * 15,
         out_specs=[pl.BlockSpec(memory_space=vm)] * 7,
         scratch_shapes=scratch,
         compiler_params=pltpu.CompilerParams(collective_id=0, has_side_effects=True, vmem_limit_bytes=62 * 2**20),

time: 206 us -> 197 us (0.956)
  Pallas kernels: 202 us -> 194 us
    pallas_call x1, Pallas kernels: 199 us -> 191 us  [local_fast(): pl.pallas_call(fast_kernel, out_shape=[shape((128, D), BF), shape((128, D...]
where the time goes in v4:
time: 197 us
  Pallas kernels  194 us (98%)
  local copies, waits for them, and re-layouts  2.13 us (1%)
    pallas_call x1, Pallas kernels, local_fast(): pl.pallas_call(fast_kernel, out_shape=[shape((128, D), BF), shape((128, D...  191 us

profile of v4, /device:TPU:0, one launch (start us, length us, event | category | flops | bytes accessed | tf_op | source)
XLA Modules:
  0.0 197.2 jit_solution(534354042647650772)
XLA Ops:
  0.6 0.0 copy-start.1
  1.3 0.0 copy-done.1
  1.3 0.7 copy.28.var_table_h
  2.0 190.9 %shard_map.246 = (bf16[128,1024]{1,0:T(8,128)(2,1)}, bf16[128,1024]{1,0:T(8,128)(2,1)}, bf16[8,32,384]{2,1,0:T(8,128)(2,1)}, bf16[32,1024]{1,0:T(8,128)(2,1)}, b...) custom-call(bf16[128,1024]{1,0:T(8,128)(2,1)} %bitcast.8, s32[1,1]{1,0:T(1,128)} %bitcast.7.lead_hours_h, ...), custom_call_target="tpu_custom_call" | custom-call | flops 14000000000 | bytes 4000000 | tf_op jit(solution)/shard_map/pallas_call | solution.py:1252
  193.0 2.8 %shard_map.247 = (bf16[1,128,1024]{2,1,0:T(8,128)(2,1)}, f32[1,128,1024]{2,1,0:T(8,128)}, f32[48,32]{1,0:T(8,128)}, f32[1,32]{1,0:T(1,128)}, f32[2,32]{1,0:T(2,1...) custom-call(bf16[128,1024]{1,0:T(8,128)(2,1)} %get-tuple-element.33., ...), custom_call_target="tpu_custom_call" | custom-call | flops 1000000 | bytes 4000000 | tf_op jit(solution)/shard_map/pallas_call | solution.py:1267
  195.7 0.0 copy-start
  195.7 0.7 copy-done
  196.5 0.7 copy.29
Async XLA Ops:
  0.6 0.7 copy-start.1
  195.7 0.7 copy-start

commit v5 on v4

--- a/solution.py
+++ b/solution.py
@@ -388,7 +388,7 @@
     mixed_o, tg_o, gq_o, go_o, gu_o, gd_o, small_o,
     lead_hours, var_mask, var_table, lead_weight, norm_gain, norm_shift, qv_bias, branch_bias, up_bias,
     tokens, wqkv_in, wup_in, wout_in, cot, tok_all, cot_all, n2_all, ml_all,
-    wqkv, wup, wdown, wout, raw, pack_in, pack_all, full,
+    wqkv, wup, wdown, wout, raw, square, pack_in, pack_all, full,
     normed, q_s, k_s, v_s, shares, attf, att,
     rs_s1, rs_r1, rs_s2, rs_r2, own, kept,
     middle, mgrad, act, uplow, dproj, dog, dk_acc, dv_acc,
@@ -468,7 +468,9 @@
     raw[...] = jnp.zeros_like(raw)
     for load in small_loads:
         load.wait()
-    raw[0:48, 0:32] = var_table[...].astype(F32)
+    square[...] = jnp.zeros_like(square)
+    square[0:32, 0:48] = var_table[...].astype(F32)
+    raw[0:48, 0:32] = jnp.transpose(square[...])[0:48, 0:32]
     for n, rows in ((48, norm_gain), (50, norm_shift), (52, qv_bias), (54, branch_bias)):
         raw[n : n + 2, 0:32] = rows[...].astype(F32)
     raw[56:57, 0:32] = lead_weight[...].astype(F32)
@@ -1215,7 +1217,7 @@
     mine = small
     for m in range(1, 4):
         mine = jnp.where(place == m, pltpu.roll(small, 128 - 32 * m, 1), mine)
-    table_o[...] = mine[0:48, 0:32]
+    table_o[...] = jnp.transpose(jnp.concatenate([mine[0:64], jnp.zeros((64, 128), F32)], axis=0))[0:32, 0:48]
     gain_o[...] = mine[68:70, 0:32]
     shift_o[...] = mine[70:72, 0:32]
     bias_o[...] = mine[72:74, 0:32]
@@ -1230,11 +1232,11 @@
 ):
     vm = pltpu.VMEM
     scratch = [
-        vm((1, 1), jnp.int32), vm((1, 48), jnp.int32), vm((48, 32), BF), vm((1, 32), BF), vm((2, 32), BF), vm((2, 32), BF),
+        vm((1, 1), jnp.int32), vm((1, 48), jnp.int32), vm((32, 48), BF), vm((1, 32), BF), vm((2, 32), BF), vm((2, 32), BF),
         vm((2, 32), BF), vm((2, 32), BF), vm((1, 128), BF),
         vm((128, D), BF), vm((32, 3 * D), BF), vm((32, 4 * D), BF), vm((32, D), BF), vm((128, D), BF),
         vm((D, D), BF), vm((D, D), BF), vm((D, D), BF), vm((D, D), BF),
-        vm((D, 384), BF), vm((D, FFL), BF), vm((FFL, D), BF), vm((128, D), BF), vm((80, 128), F32), vm((32, 128), BF), vm((32, 32, 128), BF), vm((64, D), F32),
+        vm((D, 384), BF), vm((D, FFL), BF), vm((FFL, D), BF), vm((128, D), BF), vm((80, 128), F32), vm((128, 128), F32), vm((32, 128), BF), vm((32, 32, 128), BF), vm((64, D), F32),
         vm((D, D), BF), vm((D, 128), BF), vm((D, 128), BF), vm((D, 128), BF), vm((2, D, D), BF), vm((D, 128), F32), vm((D, 128), BF),
         vm((4, 4, 128, D), BF), vm((4, 4, 128, D), BF), vm((4, 3, 128, D), BF), vm((4, 3, 128, D), BF), vm((4, 128, D), F32), vm((4, 2, 64, D), F32),
         vm((128, D), F32), vm((128, D), F32), vm((D, FFL), BF), vm((D, FFL), BF), vm((D, 384), BF), vm((D, 128), BF), vm((D, 128), F32), vm((D, 128), F32),
@@ -1261,13 +1263,13 @@
         compiler_params=pltpu.CompilerParams(collective_id=0, has_side_effects=True, vmem_limit_bytes=62 * 2**20),
         cost_estimate=pl.CostEstimate(flops=14_000_000_000, bytes_accessed=4_000_000, transcendentals=6_000_000),
     )(
-        tokens[0], lead_hours[None], var_mask, var_table, lead_weight[None], norm_gain, norm_shift, w_qkv, qv_bias, w_out,
+        tokens[0], lead_hours[None], var_mask, var_table.T, lead_weight[None], norm_gain, norm_shift, w_qkv, qv_bias, w_out,
         branch_bias, w_up, up_bias[None], w_down, cotangent[0],
     )
     out = pl.pallas_call(
         finish_kernel,
         out_shape=[
-            shape((1, 128, D), BF), shape((1, 128, D), F32), shape((48, 32), F32), shape((1, 32), F32), shape((2, 32), F32),
+            shape((1, 128, D), BF), shape((1, 128, D), F32), shape((32, 48), F32), shape((1, 32), F32), shape((2, 32), F32),
             shape((2, 32), F32), shape((32, 3 * D), F32), shape((2, 32), F32), shape((32, D), F32), shape((2, 32), F32),
             shape((32, 4 * D), F32), shape((1, 128), F32), shape((128, D), F32),
         ],
@@ -1277,7 +1279,7 @@
         cost_estimate=pl.CostEstimate(flops=1_000_000, bytes_accessed=4_000_000, transcendentals=0),
     )(*raw)
     mixed, tg, table, lead, gain, shift, gq, qv, go, bias, gu, upb, gd = out
-    return (mixed, tg, table, lead[0], gain, shift, gq, qv, go, bias, gu, upb[0], gd)
+    return (mixed, tg, table.T, lead[0], gain, shift, gq, qv, go, bias, gu, upb[0], gd)
 
 
 def solution(mesh):

time: 197 us -> 195 us (0.990)
  local copies, waits for them, and re-layouts: 2.13 us -> 0 us
    unnamed x6 -> x0, local copies, waits for them, and re-layouts: 2.13 us -> none
where the time goes in v5:
time: 195 us
  Pallas kernels  194 us (99%)
    pallas_call x1, Pallas kernels, local_fast(): pl.pallas_call(fast_kernel, out_shape=[shape((128, D), BF), shape((128, D...  191 us

profile of v5, /device:TPU:0, one launch (start us, length us, event | category | flops | bytes accessed | tf_op | source)
XLA Modules:
  0.0 195.3 jit_solution(8478541920014521620)
XLA Ops:
  1.3 191.2 %shard_map.246 = (bf16[128,1024]{1,0:T(8,128)(2,1)}, bf16[128,1024]{1,0:T(8,128)(2,1)}, bf16[8,32,384]{2,1,0:T(8,128)(2,1)}, bf16[32,1024]{1,0:T(8,128)(2,1)}, b...) custom-call(bf16[128,1024]{1,0:T(8,128)(2,1)} %bitcast.10, s32[1,1]{1,0:T(1,128)} %bitcast.9.lead_hours_h, ...), custom_call_target="tpu_custom_call" | custom-call | flops 14000000000 | bytes 4000000 | tf_op jit(solution)/shard_map/pallas_call | solution.py:1254
  192.5 2.8 %shard_map.247 = (bf16[1,128,1024]{2,1,0:T(8,128)(2,1)}, f32[1,128,1024]{2,1,0:T(8,128)}, f32[32,48]{1,0:T(8,128)}, f32[1,32]{1,0:T(1,128)}, f32[2,32]{1,0:T(2,1...) custom-call(bf16[128,1024]{1,0:T(8,128)(2,1)} %get-tuple-element.33., ...), custom_call_target="tpu_custom_call" | custom-call | flops 1000000 | bytes 4000000 | tf_op jit(solution)/shard_map/pallas_call | solution.py:1269

commit v6 on v5

--- a/solution.py
+++ b/solution.py
@@ -894,9 +894,9 @@
 
     tok.wait()
 
-    @pl.loop(0, 8)
+    @pl.loop(0, 4)
     def _(n):
-        rows = many(128 * n, 128)
+        rows = many(256 * n, 256)
         xhat, _ = center(tok_all[rows, :].astype(F32) + extra)
         normed[rows, :] = (xhat * gain0 + shift0).astype(BF)
 
@@ -964,9 +964,9 @@
 
     upb_g[...] = jnp.zeros_like(upb_g)
 
-    @pl.loop(0, 4)
+    @pl.loop(0, 2)
     def _(n):
-        rows = many(256 * n, 256)
+        rows = many(512 * n, 512)
         up = dot_nn(n2_all[rows, :], wup[...]) + bias_up
         cdf = 0.5 * (1.0 + erf(up * 0.7071067811865476))
         act[rows, :] = (up * cdf).astype(BF)
@@ -986,6 +986,8 @@
     down_red = Reduce(gdown, xdown, zdown_s, zdown)
     down_red.start()
     rs_n2.pass_on()
+    rs_mix = Scatter(2, lambda l_: dot_nn(act[rows_of(l_), :], wdown[...]))
+    rs_mix.start()
     upb_sends = Batch([(upb_g.at[:, many(128 * partner(d)[2], 128)], r_upb.at[n], partner(d)[3]) for n, d in enumerate(ranks)])
     upb_sends.start()
 
@@ -997,8 +999,6 @@
     up_red = Reduce(gup, xup, zup_s, zup)
     up_red.start()
 
-    rs_mix = Scatter(2, lambda l_: dot_nn(act[rows_of(l_), :], wdown[...]))
-    rs_mix.start()
     n2_grad = rs_n2.wait()
     incoming = cot_all[my_rows, :].astype(F32)
     xhat2, rstd2 = center(middle[...])

time: 195 us -> 193 us (0.990)
  Pallas kernels: 194 us -> 192 us
    pallas_call x1, Pallas kernels: 191 us -> 189 us  [local_fast(): pl.pallas_call(fast_kernel, out_shape=[shape((128, D), BF), shape((128, D...]
where the time goes in v6:
time: 193 us
  Pallas kernels  192 us (99%)
    pallas_call x1, Pallas kernels, local_fast(): pl.pallas_call(fast_kernel, out_shape=[shape((128, D), BF), shape((128, D...  189 us

profile of v6, /device:TPU:0, one launch (start us, length us, event | category | flops | bytes accessed | tf_op | source)
XLA Modules:
  0.0 193.2 jit_solution(6544637272537940964)
XLA Ops:
  1.3 189.1 %shard_map.246 = (bf16[128,1024]{1,0:T(8,128)(2,1)}, bf16[128,1024]{1,0:T(8,128)(2,1)}, bf16[8,32,384]{2,1,0:T(8,128)(2,1)}, bf16[32,1024]{1,0:T(8,128)(2,1)}, b...) custom-call(bf16[128,1024]{1,0:T(8,128)(2,1)} %bitcast.10, s32[1,1]{1,0:T(1,128)} %bitcast.9.lead_hours_h, ...), custom_call_target="tpu_custom_call" | custom-call | flops 14000000000 | bytes 4000000 | tf_op jit(solution)/shard_map/pallas_call | solution.py:1254
  190.4 2.8 %shard_map.247 = (bf16[1,128,1024]{2,1,0:T(8,128)(2,1)}, f32[1,128,1024]{2,1,0:T(8,128)}, f32[32,48]{1,0:T(8,128)}, f32[1,32]{1,0:T(1,128)}, f32[2,32]{1,0:T(2,1...) custom-call(bf16[128,1024]{1,0:T(8,128)(2,1)} %get-tuple-element.33., ...), custom_call_target="tpu_custom_call" | custom-call | flops 1000000 | bytes 4000000 | tf_op jit(solution)/shard_map/pallas_call | solution.py:1269
